TPU v7x, 128 devices: a whole 4x4x4 slice. The times are simulated.
128 devices in a mesh: tm: 32 (over x, z, y_hi), head: 4 (over y_lo, core).
Axes of the slice: x: 4, y: 4 (y_hi: 2, y_lo: 2; y = y_hi * 2 + y_lo), z: 4, core: 2. Of those that a mesh axis runs over, the one named last changes fastest.
Arguments:
- queries: bfloat16 [12288, 1536], P(('tm', 'head')), may hold values from -60 to 60
- keys: bfloat16 [12288, 1536], P(('tm', 'head')), may hold values from -60 to 60
- values: bfloat16 [12288, 1536], P(('tm', 'head')), may hold values from -6 to 6
- out_grad: bfloat16 [12288, 1536], P(('tm', 'head')), may hold values from -6 to 6
- window: int32 [32, 27], replicated, may hold values from 0 to 1, as said below
Outputs:
- attended: bfloat16 [12288, 1536], P(('tm', 'head'))
- query_grad: bfloat16 [12288, 1536], P(('tm', 'head'))
- key_grad: bfloat16 [12288, 1536], P(('tm', 'head'))
- value_grad: bfloat16 [12288, 1536], P(('tm', 'head'))
Inputs may be any that keep to these rules, and one draw needn't show every extreme that they name: `window`: entry 9 (a + 1) + 3 (b + 1) + (c + 1) of row s refers to the key tile at offset a in time, b in height and c in width from tile s; it is 1 for a = b = c = 0, and 0 where that tile lies outside the grid of 4 x 2 x 4 tiles.
All inputs are finite; a program needn't handle non-finite values.
Results may differ from a plain program's by a relative error of at most 0.009.
Values may be sent and summed in bfloat16 or wider, within the bound.
A program may use at most 192 MiB of HBM per device.

v0:
```python
import jax
import jax.numpy as jnp
from jax import lax
from jax.sharding import PartitionSpec as P

TILE = 384
GH = 2
GW = 4
HD = 128


EPSILON = 1e-06
OFFSETS = [
    (step_time, step_high, step_wide)
    for step_time in (-1, 0, 1)
    for step_high in (-1, 0, 1)
    for step_wide in (-1, 0, 1)
]


def from_behind(value, axis, steps):
    count = lax.axis_size(axis)
    leading, last = (max(0, -steps), min(count, count - steps))
    return lax.ppermute(value, axis, [(source, source + steps) for source in range(leading, last)])


def normed(raw_rows):
    widen_rows = raw_rows.astype(jnp.float32)
    inverse = lax.rsqrt(jnp.mean(widen_rows * widen_rows, axis=-1, keepdims=True) + EPSILON)
    return (widen_rows * inverse).astype(jnp.bfloat16)


def norm_back(raw_rows, grad_in):
    widen_rows = raw_rows.astype(jnp.float32)
    inverse = lax.rsqrt(jnp.mean(widen_rows * widen_rows, axis=-1, keepdims=True) + EPSILON)
    unit_rows = widen_rows * inverse
    return inverse * (grad_in - unit_rows * jnp.mean(grad_in * unit_rows, axis=-1, keepdims=True))


def flat_step(offset):
    return offset[0] * GH * GW + offset[1] * GW + offset[2]


def reachable(offset, grid_rows):
    return abs(offset[0]) < grid_rows and abs(offset[1]) < GH and (abs(offset[2]) < GW)


def inside_grid(coords, offset, grid_rows):
    row_pos = coords[0] + offset[0]
    high_pos = coords[1] + offset[1]
    wide_pos = coords[2] + offset[2]
    found = (
        (row_pos >= 0)
        & (row_pos < grid_rows)
        & (high_pos >= 0)
        & (high_pos < GH)
        & (wide_pos >= 0)
        & (wide_pos < GW)
    )
    return found.astype(jnp.float32)


def fetch_pair(packed, amount):
    return from_behind(packed, "tm", amount)


def send_terms(packed, amount):
    return from_behind(packed, "tm", amount)


def tile_weights(query_tile, key_tile, mask_value):
    scores = jnp.einsum(
        "qhd,khd->qhk", query_tile, key_tile, preferred_element_type=jnp.float32
    ) * HD ** (-0.5)
    return jnp.exp(scores) * mask_value


def back_terms(weights, totals, row_dot, grad_in, value_tile):
    attn_probs = weights / totals[:, :, None]
    prob_grad = jnp.einsum("qhd,khd->qhk", grad_in, value_tile, preferred_element_type=jnp.float32)
    score_grad = (attn_probs * (prob_grad - row_dot[:, :, None]) * HD ** (-0.5)).astype(
        jnp.bfloat16
    )
    return (attn_probs.astype(jnp.bfloat16), score_grad)


def key_terms(score_grad, prob_low, query_tile, grad_in):
    key_part = jnp.einsum(
        "qhk,qhd->khd", score_grad, query_tile, preferred_element_type=jnp.float32
    )
    value_part = jnp.einsum("qhk,qhd->khd", prob_low, grad_in, preferred_element_type=jnp.float32)
    return (key_part, value_part)


def shards(queries, keys, values, out_grad, window):
    regrouped = (
        lax.all_to_all(queries, "head", split_axis=1, concat_axis=0, tiled=True),
        lax.all_to_all(keys, "head", split_axis=1, concat_axis=0, tiled=True),
        lax.all_to_all(values, "head", split_axis=1, concat_axis=0, tiled=True),
        lax.all_to_all(out_grad, "head", split_axis=1, concat_axis=0, tiled=True),
    )
    query_raw, key_raw, value_tile, grad_tile = [piece.reshape(TILE, -1, HD) for piece in regrouped]
    query_unit = normed(query_raw)
    key_unit = normed(key_raw)
    position = lax.axis_index("tm")
    tile_total = lax.axis_size("tm")
    grid_rows = tile_total // (GH * GW)
    coords = (position // (GH * GW), position // GW % GH, position % GW)
    used = [slot for slot in range(27) if reachable(OFFSETS[slot], grid_rows)]
    own_row = lax.dynamic_index_in_dim(window, position, 0, keepdims=False).astype(jnp.float32)
    valid = {slot: inside_grid(coords, OFFSETS[slot], grid_rows) for slot in used}
    masks = {slot: own_row[slot] * valid[slot] for slot in used}
    pair = jnp.stack([key_unit, value_tile], 0)
    key_cands = {}
    value_cands = {}
    for slot in used:
        near = pair if slot == 13 else fetch_pair(pair, -flat_step(OFFSETS[slot]))
        key_cands[slot] = near[0]
        value_cands[slot] = near[1]
    head_count = query_unit.shape[1]
    totals = jnp.zeros((TILE, head_count), jnp.float32)
    mixed = jnp.zeros((TILE, head_count, HD), jnp.float32)
    for slot in used:
        weights = tile_weights(query_unit, key_cands[slot], masks[slot])
        totals = totals + jnp.sum(weights, axis=-1)
        mixed = mixed + jnp.einsum(
            "qhk,khd->qhd",
            weights.astype(jnp.bfloat16),
            value_cands[slot],
            preferred_element_type=jnp.float32,
        )
    output = (mixed / totals[:, :, None]).astype(jnp.bfloat16)
    row_dot = jnp.sum(grad_tile.astype(jnp.float32) * output.astype(jnp.float32), axis=-1)
    dquery = jnp.zeros((TILE, head_count, HD), jnp.float32)
    key_total = jnp.zeros((TILE, head_count, HD), jnp.float32)
    value_total = jnp.zeros((TILE, head_count, HD), jnp.float32)
    for slot in used:
        weights = tile_weights(query_unit, key_cands[slot], masks[slot])
        prob_low, score_grad = back_terms(weights, totals, row_dot, grad_tile, value_cands[slot])
        dquery = dquery + jnp.einsum(
            "qhk,khd->qhd", score_grad, key_cands[slot], preferred_element_type=jnp.float32
        )
        if slot == 13:
            key_part, value_part = key_terms(score_grad, prob_low, query_unit, grad_tile)
            key_total = key_total + key_part
            value_total = value_total + value_part
        else:
            key_part, value_part = key_terms(score_grad, prob_low, query_unit, grad_tile)
            arrived = send_terms(
                jnp.stack([key_part, value_part], 0).astype(jnp.bfloat16), flat_step(OFFSETS[slot])
            )
            key_total = key_total + arrived[0].astype(jnp.float32)
            value_total = value_total + arrived[1].astype(jnp.float32)
    query_grad = norm_back(query_raw, dquery).astype(jnp.bfloat16)
    key_grad = norm_back(key_raw, key_total).astype(jnp.bfloat16)
    value_grad = value_total.astype(jnp.bfloat16)
    flat_out = output.reshape(TILE, -1)
    flat_query = query_grad.reshape(TILE, -1)
    flat_key = key_grad.reshape(TILE, -1)
    flat_value = value_grad.reshape(TILE, -1)
    return (
        lax.all_to_all(flat_out, "head", split_axis=0, concat_axis=1, tiled=True),
        lax.all_to_all(flat_query, "head", split_axis=0, concat_axis=1, tiled=True),
        lax.all_to_all(flat_key, "head", split_axis=0, concat_axis=1, tiled=True),
        lax.all_to_all(flat_value, "head", split_axis=0, concat_axis=1, tiled=True),
    )


def solution(mesh):
    return jax.shard_map(
        shards,
        mesh=mesh,
        in_specs=(
            P(("tm", "head"), None),
            P(("tm", "head"), None),
            P(("tm", "head"), None),
            P(("tm", "head"), None),
            P(),
        ),
        out_specs=(
            P(("tm", "head"), None),
            P(("tm", "head"), None),
            P(("tm", "head"), None),
            P(("tm", "head"), None),
        ),
        check_vma=False,
    )
```

profile of v0, /device:TPU:100, one launch (start us, length us, event | category | flops | bytes accessed | tf_op | source)
XLA Modules:
  0.0 846.5 jit_solution(10821369115356824102)
XLA Ops:
  2.4 3.5 all-to-all-start.2
  28.1 3.5 all-to-all-start
  32.6 5.3 all-to-all-done
  37.9 3.5 all-to-all-start.1
  42.5 5.2 all-to-all-done.1
  47.7 4.1 all-to-all-start.4
  53.1 4.4 collective-permute-start.8
  57.4 6.0 collective-permute-start.6
  63.4 3.6 collective-permute-start.9
  76.2 60.1 %collective-permute-done.9 = bf16[2,384,3,128]{3,1,2,0:T(8,128)(2,1)} collective-permute-done((bf16[2,384,3,128]{3,1,2,0:T(8,128)(2,1)}, bf16[2,384,3,128]{3,1,2,0:T(8,128)(2,1)}, u32[]{:S(2)}, u32[]{:S(2)}) %collective-permute-start.9) | collective-permute-done | bytes 589856 | tf_op jit(solution)/shard_map/ppermute | solution.py:24
  139.6 5.4 collective-permute-start.5
  149.8 8.1 collective-permute-done.3
  159.7 16.8 %collective-permute-done.5 = bf16[2,384,3,128]{3,1,2,0:T(8,128)(2,1)S(1)} collective-permute-done((bf16[2,384,3,128]{3,1,2,0:T(8,128)(2,1)}, bf16[2,384,3,128]{3,1,2,0:T(8,128)(2,1)S(1)}, u32[]{:S(2)}, u32[]{:S(2)}) %collective-permute-start.5) | collective-permute-done | bytes 589856 | tf_op jit(solution)/shard_map/ppermute | solution.py:24
  178.9 9.2 %collective-permute-done.4 = bf16[2,384,3,128]{3,1,2,0:T(8,128)(2,1)S(1)} collective-permute-done((bf16[2,384,3,128]{3,1,2,0:T(8,128)(2,1)}, bf16[2,384,3,128]{3,1,2,0:T(8,128)(2,1)S(1)}, u32[]{:S(2)}, u32[]{:S(2)}) %collective-permute-start.4) | collective-permute-done | bytes 589856 | tf_op jit(solution)/shard_map/ppermute | solution.py:24
  188.1 7.9 collective-permute-start.16
  200.2 25.5 %collective-permute-done.10 = bf16[2,384,3,128]{3,1,2,0:T(8,128)(2,1)S(1)} collective-permute-done((bf16[2,384,3,128]{3,1,2,0:T(8,128)(2,1)}, bf16[2,384,3,128]{3,1,2,0:T(8,128)(2,1)S(1)}, u32[]{:S(2)}, u32[]{:S(2)}) %collective-permute-start.10) | collective-permute-done | bytes 589856 | tf_op jit(solution)/shard_map/ppermute | solution.py:24
  231.7 12.2 %collective-permute-done.15 = bf16[2,384,3,128]{3,1,2,0:T(8,128)(2,1)S(1)} collective-permute-done((bf16[2,384,3,128]{3,1,2,0:T(8,128)(2,1)}, bf16[2,384,3,128]{3,1,2,0:T(8,128)(2,1)S(1)}, u32[]{:S(2)}, u32[]{:S(2)}) %collective-permute-start.15) | collective-permute-done | bytes 589856 | tf_op jit(solution)/shard_map/ppermute | solution.py:24
  243.9 37.2 %collective-permute-start.19 = (bf16[2,384,3,128]{3,1,2,0:T(8,128)(2,1)}, bf16[2,384,3,128]{3,1,2,0:T(8,128)(2,1)S(1)}, u32[]{:S(2)}, u32[]{:S(2)}) collective-permute-start(bf16[2,384,3,128]{3,1,2,0:T(8,128)(2,1)} %pad_maximum_fusion), channel_id=1, source_target_pairs={{52,0},{56,4},{60,8},{64,12},{68,16},{72,20},{76,24},{80,28},{84,3... | collective-permute-start | bytes 1769480 | tf_op jit(solution)/shard_map/ppermute | solution.py:24
  284.0 19.7 %collective-permute-done.18 = bf16[2,384,3,128]{3,1,2,0:T(8,128)(2,1)S(1)} collective-permute-done((bf16[2,384,3,128]{3,1,2,0:T(8,128)(2,1)}, bf16[2,384,3,128]{3,1,2,0:T(8,128)(2,1)S(1)}, u32[]{:S(2)}, u32[]{:S(2)}) %collective-permute-start.18) | collective-permute-done | bytes 589856 | tf_op jit(solution)/shard_map/ppermute | solution.py:24
  306.1 19.2 %collective-permute-done.19 = bf16[2,384,3,128]{3,1,2,0:T(8,128)(2,1)S(1)} collective-permute-done((bf16[2,384,3,128]{3,1,2,0:T(8,128)(2,1)}, bf16[2,384,3,128]{3,1,2,0:T(8,128)(2,1)S(1)}, u32[]{:S(2)}, u32[]{:S(2)}) %collective-permute-start.19) | collective-permute-done | bytes 589856 | tf_op jit(solution)/shard_map/ppermute | solution.py:24
  325.3 4.8 collective-permute-start.13
  336.1 18.9 %collective-permute-done.13 = bf16[2,384,3,128]{3,1,2,0:T(8,128)(2,1)S(1)} collective-permute-done((bf16[2,384,3,128]{3,1,2,0:T(8,128)(2,1)}, bf16[2,384,3,128]{3,1,2,0:T(8,128)(2,1)S(1)}, u32[]{:S(2)}, u32[]{:S(2)}) %collective-permute-start.13) | collective-permute-done | bytes 589856 | tf_op jit(solution)/shard_map/ppermute | solution.py:24
  355.6 3.4 collective-permute-done.12
  428.4 9.6 %collective-permute-start.20 = (bf16[2,384,3,128]{1,3,2,0:T(8,128)(2,1)}, bf16[2,384,3,128]{1,3,2,0:T(8,128)(2,1)}, u32[]{:S(2)}, u32[]{:S(2)}) collective-permute-start(bf16[2,384,3,128]{1,3,2,0:T(8,128)(2,1)} %pad_maximum_fusion.1), channel_id=1, source_target_pairs={{52,0},{56,4},{60,8},{64,12},{68,16},{72,20},{76,24},{80,28},{84,3... | collective-permute-start | bytes 1769480 | tf_op jit(solution)/shard_map/ppermute | solution.py:24
  461.3 6.5 multiply_convert_fusion.11
  519.1 5.0 collective-permute-done.24
  526.0 8.2 collective-permute-done.25
  537.8 5.3 collective-permute-done.26
  543.1 4.5 collective-permute-start.31
  547.6 42.2 %collective-permute-done.27 = bf16[2,384,3,128]{1,3,2,0:T(8,128)(2,1)S(1)} collective-permute-done((bf16[2,384,3,128]{1,3,2,0:T(8,128)(2,1)S(1)}, bf16[2,384,3,128]{1,3,2,0:T(8,128)(2,1)S(1)}, u32[]{:S(2)}, u32[]{:S(2)}) %collective-permute-start.27) | collective-permute-done | bytes 589856 | tf_op jit(solution)/shard_map/ppermute | solution.py:24
  589.8 9.3 %collective-permute-start.32 = (bf16[2,384,3,128]{1,3,2,0:T(8,128)(2,1)S(1)}, bf16[2,384,3,128]{1,3,2,0:T(8,128)(2,1)S(1)}, u32[]{:S(2)}, u32[]{:S(2)}) collective-permute-start(bf16[2,384,3,128]{1,3,2,0:T(8,128)(2,1)S(1)} %pad_maximum_fusion.13), channel_id=1, source_target_pairs={{4,0},{8,4},{12,8},{16,12},{20,16},{24,20},{28,24},{32,28},{36,32}... | collective-permute-start | bytes 1769480 | tf_op jit(solution)/shard_map/ppermute | solution.py:24
  599.2 6.5 collective-permute-start.33
  607.7 36.5 %collective-permute-done.30 = bf16[2,384,3,128]{1,3,2,0:T(8,128)(2,1)S(1)} collective-permute-done((bf16[2,384,3,128]{1,3,2,0:T(8,128)(2,1)S(1)}, bf16[2,384,3,128]{1,3,2,0:T(8,128)(2,1)S(1)}, u32[]{:S(2)}, u32[]{:S(2)}) %collective-permute-start.30) | collective-permute-done | bytes 589856 | tf_op jit(solution)/shard_map/ppermute | solution.py:24
  650.9 11.6 %collective-permute-start.38 = (bf16[2,384,3,128]{1,3,2,0:T(8,128)(2,1)S(1)}, bf16[2,384,3,128]{1,3,2,0:T(8,128)(2,1)S(1)}, u32[]{:S(2)}, u32[]{:S(2)}) collective-permute-start(bf16[2,384,3,128]{1,3,2,0:T(8,128)(2,1)S(1)} %pad_maximum_fusion.19), channel_id=1, source_target_pairs={{0,16},{4,20},{8,24},{12,28},{16,32},{20,36},{24,40},{28,44},{32,4... | collective-permute-start | bytes 1769480 | tf_op jit(solution)/shard_map/ppermute | solution.py:24
  662.5 4.9 collective-permute-done.34
  669.3 47.2 %collective-permute-done.35 = bf16[2,384,3,128]{1,3,2,0:T(8,128)(2,1)S(1)} collective-permute-done((bf16[2,384,3,128]{1,3,2,0:T(8,128)(2,1)S(1)}, bf16[2,384,3,128]{1,3,2,0:T(8,128)(2,1)S(1)}, u32[]{:S(2)}, u32[]{:S(2)}) %collective-permute-start.35) | collective-permute-done | bytes 589856 | tf_op jit(solution)/shard_map/ppermute | solution.py:24
  723.9 3.5 collective-permute-done.38
  730.0 12.2 %collective-permute-done.40 = bf16[2,384,3,128]{1,3,2,0:T(8,128)(2,1)S(1)} collective-permute-done((bf16[2,384,3,128]{1,3,2,0:T(8,128)(2,1)S(1)}, bf16[2,384,3,128]{1,3,2,0:T(8,128)(2,1)S(1)}, u32[]{:S(2)}, u32[]{:S(2)}) %collective-permute-start.40) | collective-permute-done | bytes 589856 | tf_op jit(solution)/shard_map/ppermute | solution.py:24
  748.0 35.7 %all-to-all-start.5 = ((bf16[4,96,384]{2,1,0:T(8,128)(2,1)}), bf16[4,96,384]{2,1,0:T(8,128)(2,1)}, u32[]{:S(2)}, u32[]{:S(2)}) async-start(bf16[4,96,384]{2,1,0:T(8,128)(2,1)} %copy.1684), calls=%async_computation.5 | async-start | bytes 589824 | tf_op jit(solution)/shard_map/all_to_all | solution.py:163
  786.1 6.2 collective-permute-done.44
  792.3 14.6 %collective-permute-done.45 = bf16[2,384,3,128]{1,3,2,0:T(8,128)(2,1)} collective-permute-done((bf16[2,384,3,128]{1,3,2,0:T(8,128)(2,1)}, bf16[2,384,3,128]{1,3,2,0:T(8,128)(2,1)}, u32[]{:S(2)}, u32[]{:S(2)}) %collective-permute-start.45) | collective-permute-done | bytes 589856 | tf_op jit(solution)/shard_map/ppermute | solution.py:24
  806.9 4.4 fusion.225
  815.9 3.5 all-to-all-start.3
  819.3 6.3 all-to-all-done.3
  825.7 3.5 all-to-all-start.7
  830.5 5.0 all-to-all-done.7
  835.5 3.5 all-to-all-start.6
  842.1 3.2 all-to-all-done.6
  (519 shorter events, 239.9 us)
Async XLA Ops:
  2.4 25.6 %all-to-all-start.2 = ((bf16[96,4,384]{2,0,1:T(8,128)(2,1)}), bf16[96,4,384]{2,0,1:T(8,128)(2,1)S(1)}, u32[]{:S(2)}, u32[]{:S(2)}) async-start(bf16[96,4,384]{2,0,1:T(8,128)(2,1)} %bitcast.1469), calls=%async_computation.2 | async-start | bytes 589824 | tf_op jit(solution)/shard_map/all_to_all | solution.py:97
  47.7 26.9 %all-to-all-start.4 = ((bf16[96,4,384]{2,0,1:T(8,128)(2,1)}), bf16[96,4,384]{2,0,1:T(8,128)(2,1)}, u32[]{:S(2)}, u32[]{:S(2)}) async-start(bf16[96,4,384]{2,0,1:T(8,128)(2,1)} %bitcast.1468), calls=%async_computation.4 | async-start | bytes 589824 | tf_op jit(solution)/shard_map/all_to_all | solution.py:100
  53.1 277.5 %collective-permute-start.8 = (bf16[2,384,3,128]{3,1,2,0:T(8,128)(2,1)}, bf16[2,384,3,128]{3,1,2,0:T(8,128)(2,1)S(1)}, u32[]{:S(2)}, u32[]{:S(2)}) collective-permute-start(bf16[2,384,3,128]{3,1,2,0:T(8,128)(2,1)} %pad_maximum_fusion), channel_id=1, source_target_pairs={{0,12},{4,16},{8,20},{12,24},{16,28},{20,32},{24,36},{28,40},{32,4... | collective-permute-start | bytes 1769480 | tf_op jit(solution)/shard_map/ppermute | solution.py:24
  57.4 275.9 %collective-permute-start.6 = (bf16[2,384,3,128]{3,1,2,0:T(8,128)(2,1)}, bf16[2,384,3,128]{3,1,2,0:T(8,128)(2,1)}, u32[]{:S(2)}, u32[]{:S(2)}) collective-permute-start(bf16[2,384,3,128]{3,1,2,0:T(8,128)(2,1)} %pad_maximum_fusion), channel_id=1, source_target_pairs={{0,20},{4,24},{8,28},{12,32},{16,36},{20,40},{24,44},{28,48},{32,5... | collective-permute-start | bytes 1769480 | tf_op jit(solution)/shard_map/ppermute | solution.py:24
  63.4 72.8 %collective-permute-start.9 = (bf16[2,384,3,128]{3,1,2,0:T(8,128)(2,1)}, bf16[2,384,3,128]{3,1,2,0:T(8,128)(2,1)}, u32[]{:S(2)}, u32[]{:S(2)}) collective-permute-start(bf16[2,384,3,128]{3,1,2,0:T(8,128)(2,1)} %pad_maximum_fusion), channel_id=1, source_target_pairs={{0,4},{4,8},{8,12},{12,16},{16,20},{20,24},{24,28},{28,32},{32,36}... | collective-permute-start | bytes 1769480 | tf_op jit(solution)/shard_map/ppermute | solution.py:24
  67.1 72.6 %collective-permute-start.2 = (bf16[2,384,3,128]{3,1,2,0:T(8,128)(2,1)}, bf16[2,384,3,128]{3,1,2,0:T(8,128)(2,1)}, u32[]{:S(2)}, u32[]{:S(2)}) collective-permute-start(bf16[2,384,3,128]{3,1,2,0:T(8,128)(2,1)} %pad_maximum_fusion), channel_id=1, source_target_pairs={{0,44},{4,48},{8,52},{12,56},{16,60},{20,64},{24,68},{28,72},{32,7... | collective-permute-start | bytes 1769480 | tf_op jit(solution)/shard_map/ppermute | solution.py:24
  68.4 78.1 %collective-permute-start.1 = (bf16[2,384,3,128]{3,1,2,0:T(8,128)(2,1)}, bf16[2,384,3,128]{3,1,2,0:T(8,128)(2,1)}, u32[]{:S(2)}, u32[]{:S(2)}) collective-permute-start(bf16[2,384,3,128]{3,1,2,0:T(8,128)(2,1)} %pad_maximum_fusion), channel_id=1, source_target_pairs={{0,48},{4,52},{8,56},{12,60},{16,64},{20,68},{24,72},{28,76},{32,8... | collective-permute-start | bytes 1769480 | tf_op jit(solution)/shard_map/ppermute | solution.py:24
  136.3 21.6 %collective-permute-start.3 = (bf16[2,384,3,128]{3,1,2,0:T(8,128)(2,1)}, bf16[2,384,3,128]{3,1,2,0:T(8,128)(2,1)S(1)}, u32[]{:S(2)}, u32[]{:S(2)}) collective-permute-start(bf16[2,384,3,128]{3,1,2,0:T(8,128)(2,1)} %pad_maximum_fusion), channel_id=1, source_target_pairs={{0,36},{4,40},{8,44},{12,48},{16,52},{20,56},{24,60},{28,64},{32,6... | collective-permute-start | bytes 1769480 | tf_op jit(solution)/shard_map/ppermute | solution.py:24
  139.6 36.9 %collective-permute-start.5 = (bf16[2,384,3,128]{3,1,2,0:T(8,128)(2,1)}, bf16[2,384,3,128]{3,1,2,0:T(8,128)(2,1)S(1)}, u32[]{:S(2)}, u32[]{:S(2)}) collective-permute-start(bf16[2,384,3,128]{3,1,2,0:T(8,128)(2,1)} %pad_maximum_fusion), channel_id=1, source_target_pairs={{0,28},{4,32},{8,36},{12,40},{16,44},{20,48},{24,52},{28,56},{32,6... | collective-permute-start | bytes 1769480 | tf_op jit(solution)/shard_map/ppermute | solution.py:24
  146.5 41.7 %collective-permute-start.4 = (bf16[2,384,3,128]{3,1,2,0:T(8,128)(2,1)}, bf16[2,384,3,128]{3,1,2,0:T(8,128)(2,1)S(1)}, u32[]{:S(2)}, u32[]{:S(2)}) collective-permute-start(bf16[2,384,3,128]{3,1,2,0:T(8,128)(2,1)} %pad_maximum_fusion), channel_id=1, source_target_pairs={{0,32},{4,36},{8,40},{12,44},{16,48},{20,52},{24,56},{28,60},{32,6... | collective-permute-start | bytes 1769480 | tf_op jit(solution)/shard_map/ppermute | solution.py:24
  157.9 38.6 %collective-permute-start = (bf16[2,384,3,128]{3,1,2,0:T(8,128)(2,1)}, bf16[2,384,3,128]{3,1,2,0:T(8,128)(2,1)S(1)}, u32[]{:S(2)}, u32[]{:S(2)}) collective-permute-start(bf16[2,384,3,128]{3,1,2,0:T(8,128)(2,1)} %pad_maximum_fusion), channel_id=1, source_target_pairs={{0,52},{4,56},{8,60},{12,64},{16,68},{20,72},{24,76},{28,80},{32,8... | collective-permute-start | bytes 1769480 | tf_op jit(solution)/shard_map/ppermute | solution.py:24
  176.5 49.1 %collective-permute-start.10 = (bf16[2,384,3,128]{3,1,2,0:T(8,128)(2,1)}, bf16[2,384,3,128]{3,1,2,0:T(8,128)(2,1)S(1)}, u32[]{:S(2)}, u32[]{:S(2)}) collective-permute-start(bf16[2,384,3,128]{3,1,2,0:T(8,128)(2,1)} %pad_maximum_fusion), channel_id=1, source_target_pairs={{4,0},{8,4},{12,8},{16,12},{20,16},{24,20},{28,24},{32,28},{36,32}... | collective-permute-start | bytes 1769480 | tf_op jit(solution)/shard_map/ppermute | solution.py:24
  188.1 39.9 %collective-permute-start.16 = (bf16[2,384,3,128]{3,1,2,0:T(8,128)(2,1)}, bf16[2,384,3,128]{3,1,2,0:T(8,128)(2,1)S(1)}, u32[]{:S(2)}, u32[]{:S(2)}) collective-permute-start(bf16[2,384,3,128]{3,1,2,0:T(8,128)(2,1)} %pad_maximum_fusion), channel_id=1, source_target_pairs={{36,0},{40,4},{44,8},{48,12},{52,16},{56,20},{60,24},{64,28},{68,3... | collective-permute-start | bytes 1769480 | tf_op jit(solution)/shard_map/ppermute | solution.py:24
  196.5 33.4 %collective-permute-start.14 = (bf16[2,384,3,128]{3,1,2,0:T(8,128)(2,1)}, bf16[2,384,3,128]{3,1,2,0:T(8,128)(2,1)S(1)}, u32[]{:S(2)}, u32[]{:S(2)}) collective-permute-start(bf16[2,384,3,128]{3,1,2,0:T(8,128)(2,1)} %pad_maximum_fusion), channel_id=1, source_target_pairs={{28,0},{32,4},{36,8},{40,12},{44,16},{48,20},{52,24},{56,28},{60,3... | collective-permute-start | bytes 1769480 | tf_op jit(solution)/shard_map/ppermute | solution.py:24
  228.1 53.5 %collective-permute-start.17 = (bf16[2,384,3,128]{3,1,2,0:T(8,128)(2,1)}, bf16[2,384,3,128]{3,1,2,0:T(8,128)(2,1)S(1)}, u32[]{:S(2)}, u32[]{:S(2)}) collective-permute-start(bf16[2,384,3,128]{3,1,2,0:T(8,128)(2,1)} %pad_maximum_fusion), channel_id=1, source_target_pairs={{44,0},{48,4},{52,8},{56,12},{60,16},{64,20},{68,24},{72,28},{76,3... | collective-permute-start | bytes 1769480 | tf_op jit(solution)/shard_map/ppermute | solution.py:24
  229.9 73.8 %collective-permute-start.18 = (bf16[2,384,3,128]{3,1,2,0:T(8,128)(2,1)}, bf16[2,384,3,128]{3,1,2,0:T(8,128)(2,1)S(1)}, u32[]{:S(2)}, u32[]{:S(2)}) collective-permute-start(bf16[2,384,3,128]{3,1,2,0:T(8,128)(2,1)} %pad_maximum_fusion), channel_id=1, source_target_pairs={{48,0},{52,4},{56,8},{60,12},{64,16},{68,20},{72,24},{76,28},{80,3... | collective-permute-start | bytes 1769480 | tf_op jit(solution)/shard_map/ppermute | solution.py:24
  243.9 81.3 %collective-permute-start.19 = (bf16[2,384,3,128]{3,1,2,0:T(8,128)(2,1)}, bf16[2,384,3,128]{3,1,2,0:T(8,128)(2,1)S(1)}, u32[]{:S(2)}, u32[]{:S(2)}) collective-permute-start(bf16[2,384,3,128]{3,1,2,0:T(8,128)(2,1)} %pad_maximum_fusion), channel_id=1, source_target_pairs={{52,0},{56,4},{60,8},{64,12},{68,16},{72,20},{76,24},{80,28},{84,3... | collective-permute-start | bytes 1769480 | tf_op jit(solution)/shard_map/ppermute | solution.py:24
  281.6 53.2 %collective-permute-start.7 = (bf16[2,384,3,128]{3,1,2,0:T(8,128)(2,1)}, bf16[2,384,3,128]{3,1,2,0:T(8,128)(2,1)S(1)}, u32[]{:S(2)}, u32[]{:S(2)}) collective-permute-start(bf16[2,384,3,128]{3,1,2,0:T(8,128)(2,1)} %pad_maximum_fusion), channel_id=1, source_target_pairs={{0,16},{4,20},{8,24},{12,28},{16,32},{20,36},{24,40},{28,44},{32,4... | collective-permute-start | bytes 1769480 | tf_op jit(solution)/shard_map/ppermute | solution.py:24
  303.7 31.8 %collective-permute-start.11 = (bf16[2,384,3,128]{3,1,2,0:T(8,128)(2,1)}, bf16[2,384,3,128]{3,1,2,0:T(8,128)(2,1)S(1)}, u32[]{:S(2)}, u32[]{:S(2)}) collective-permute-start(bf16[2,384,3,128]{3,1,2,0:T(8,128)(2,1)} %pad_maximum_fusion), channel_id=1, source_target_pairs={{12,0},{16,4},{20,8},{24,12},{28,16},{32,20},{36,24},{40,28},{44,3... | collective-permute-start | bytes 1769480 | tf_op jit(solution)/shard_map/ppermute | solution.py:24
  325.3 29.7 %collective-permute-start.13 = (bf16[2,384,3,128]{3,1,2,0:T(8,128)(2,1)}, bf16[2,384,3,128]{3,1,2,0:T(8,128)(2,1)S(1)}, u32[]{:S(2)}, u32[]{:S(2)}) collective-permute-start(bf16[2,384,3,128]{3,1,2,0:T(8,128)(2,1)} %pad_maximum_fusion), channel_id=1, source_target_pairs={{20,0},{24,4},{28,8},{32,12},{36,16},{40,20},{44,24},{48,28},{52,3... | collective-permute-start | bytes 1769480 | tf_op jit(solution)/shard_map/ppermute | solution.py:24
  330.6 28.4 %collective-permute-start.12 = (bf16[2,384,3,128]{3,1,2,0:T(8,128)(2,1)}, bf16[2,384,3,128]{3,1,2,0:T(8,128)(2,1)S(1)}, u32[]{:S(2)}, u32[]{:S(2)}) collective-permute-start(bf16[2,384,3,128]{3,1,2,0:T(8,128)(2,1)} %pad_maximum_fusion), channel_id=1, source_target_pairs={{16,0},{20,4},{24,8},{28,12},{32,16},{36,20},{40,24},{44,28},{48,3... | collective-permute-start | bytes 1769480 | tf_op jit(solution)/shard_map/ppermute | solution.py:24
  428.4 80.8 %collective-permute-start.20 = (bf16[2,384,3,128]{1,3,2,0:T(8,128)(2,1)}, bf16[2,384,3,128]{1,3,2,0:T(8,128)(2,1)}, u32[]{:S(2)}, u32[]{:S(2)}) collective-permute-start(bf16[2,384,3,128]{1,3,2,0:T(8,128)(2,1)} %pad_maximum_fusion.1), channel_id=1, source_target_pairs={{52,0},{56,4},{60,8},{64,12},{68,16},{72,20},{76,24},{80,28},{84,3... | collective-permute-start | bytes 1769480 | tf_op jit(solution)/shard_map/ppermute | solution.py:24
  440.7 72.4 %collective-permute-start.21 = (bf16[2,384,3,128]{1,3,2,0:T(8,128)(2,1)}, bf16[2,384,3,128]{1,3,2,0:T(8,128)(2,1)}, u32[]{:S(2)}, u32[]{:S(2)}) collective-permute-start(bf16[2,384,3,128]{1,3,2,0:T(8,128)(2,1)} %pad_maximum_fusion.2), channel_id=1, source_target_pairs={{48,0},{52,4},{56,8},{60,12},{64,16},{68,20},{72,24},{76,28},{80,3... | collective-permute-start | bytes 1769480 | tf_op jit(solution)/shard_map/ppermute | solution.py:24
  445.7 69.6 %collective-permute-start.22 = (bf16[2,384,3,128]{1,3,2,0:T(8,128)(2,1)}, bf16[2,384,3,128]{1,3,2,0:T(8,128)(2,1)}, u32[]{:S(2)}, u32[]{:S(2)}) collective-permute-start(bf16[2,384,3,128]{1,3,2,0:T(8,128)(2,1)} %pad_maximum_fusion.3), channel_id=1, source_target_pairs={{44,0},{48,4},{52,8},{56,12},{60,16},{64,20},{68,24},{72,28},{76,3... | collective-permute-start | bytes 1769480 | tf_op jit(solution)/shard_map/ppermute | solution.py:24
  449.7 67.4 %collective-permute-start.23 = (bf16[2,384,3,128]{1,3,2,0:T(8,128)(2,1)}, bf16[2,384,3,128]{1,3,2,0:T(8,128)(2,1)}, u32[]{:S(2)}, u32[]{:S(2)}) collective-permute-start(bf16[2,384,3,128]{1,3,2,0:T(8,128)(2,1)} %pad_maximum_fusion.4), channel_id=1, source_target_pairs={{36,0},{40,4},{44,8},{48,12},{52,16},{56,20},{60,24},{64,28},{68,3... | collective-permute-start | bytes 1769480 | tf_op jit(solution)/shard_map/ppermute | solution.py:24
  453.5 70.5 %collective-permute-start.24 = (bf16[2,384,3,128]{1,3,2,0:T(8,128)(2,1)}, bf16[2,384,3,128]{1,3,2,0:T(8,128)(2,1)}, u32[]{:S(2)}, u32[]{:S(2)}) collective-permute-start(bf16[2,384,3,128]{1,3,2,0:T(8,128)(2,1)} %pad_maximum_fusion.5), channel_id=1, source_target_pairs={{32,0},{36,4},{40,8},{44,12},{48,16},{52,20},{56,24},{60,28},{64,3... | collective-permute-start | bytes 1769480 | tf_op jit(solution)/shard_map/ppermute | solution.py:24
  509.2 24.9 %collective-permute-start.25 = (bf16[2,384,3,128]{1,3,2,0:T(8,128)(2,1)S(1)}, bf16[2,384,3,128]{1,3,2,0:T(8,128)(2,1)S(1)}, u32[]{:S(2)}, u32[]{:S(2)}) collective-permute-start(bf16[2,384,3,128]{1,3,2,0:T(8,128)(2,1)S(1)} %pad_maximum_fusion.6), channel_id=1, source_target_pairs={{28,0},{32,4},{36,8},{40,12},{44,16},{48,20},{52,24},{56,28},{60,3... | collective-permute-start | bytes 1769480 | tf_op jit(solution)/shard_map/ppermute | solution.py:24
  513.1 30.0 %collective-permute-start.26 = (bf16[2,384,3,128]{1,3,2,0:T(8,128)(2,1)S(1)}, bf16[2,384,3,128]{1,3,2,0:T(8,128)(2,1)S(1)}, u32[]{:S(2)}, u32[]{:S(2)}) collective-permute-start(bf16[2,384,3,128]{1,3,2,0:T(8,128)(2,1)S(1)} %pad_maximum_fusion.7), channel_id=1, source_target_pairs={{20,0},{24,4},{28,8},{32,12},{36,16},{40,20},{44,24},{48,28},{52,3... | collective-permute-start | bytes 1769480 | tf_op jit(solution)/shard_map/ppermute | solution.py:24
  515.2 74.6 %collective-permute-start.27 = (bf16[2,384,3,128]{1,3,2,0:T(8,128)(2,1)S(1)}, bf16[2,384,3,128]{1,3,2,0:T(8,128)(2,1)S(1)}, u32[]{:S(2)}, u32[]{:S(2)}) collective-permute-start(bf16[2,384,3,128]{1,3,2,0:T(8,128)(2,1)S(1)} %pad_maximum_fusion.8), channel_id=1, source_target_pairs={{16,0},{20,4},{24,8},{28,12},{32,16},{36,20},{40,24},{44,28},{48,3... | collective-permute-start | bytes 1769480 | tf_op jit(solution)/shard_map/ppermute | solution.py:24
  517.2 82.0 %collective-permute-start.28 = (bf16[2,384,3,128]{1,3,2,0:T(8,128)(2,1)S(1)}, bf16[2,384,3,128]{1,3,2,0:T(8,128)(2,1)S(1)}, u32[]{:S(2)}, u32[]{:S(2)}) collective-permute-start(bf16[2,384,3,128]{1,3,2,0:T(8,128)(2,1)S(1)} %pad_maximum_fusion.9), channel_id=1, source_target_pairs={{12,0},{16,4},{20,8},{24,12},{28,16},{32,20},{36,24},{40,28},{44,3... | collective-permute-start | bytes 1769480 | tf_op jit(solution)/shard_map/ppermute | solution.py:24
  524.0 81.7 %collective-permute-start.29 = (bf16[2,384,3,128]{1,3,2,0:T(8,128)(2,1)S(1)}, bf16[2,384,3,128]{1,3,2,0:T(8,128)(2,1)S(1)}, u32[]{:S(2)}, u32[]{:S(2)}) collective-permute-start(bf16[2,384,3,128]{1,3,2,0:T(8,128)(2,1)S(1)} %pad_maximum_fusion.10), channel_id=1, source_target_pairs={{20,0},{24,4},{28,8},{32,12},{36,16},{40,20},{44,24},{48,28},{52,3... | collective-permute-start | bytes 1769480 | tf_op jit(solution)/shard_map/ppermute | solution.py:24
  534.2 110.0 %collective-permute-start.30 = (bf16[2,384,3,128]{1,3,2,0:T(8,128)(2,1)S(1)}, bf16[2,384,3,128]{1,3,2,0:T(8,128)(2,1)S(1)}, u32[]{:S(2)}, u32[]{:S(2)}) collective-permute-start(bf16[2,384,3,128]{1,3,2,0:T(8,128)(2,1)S(1)} %pad_maximum_fusion.11), channel_id=1, source_target_pairs={{16,0},{20,4},{24,8},{28,12},{32,16},{36,20},{40,24},{44,28},{48,3... | collective-permute-start | bytes 1769480 | tf_op jit(solution)/shard_map/ppermute | solution.py:24
  543.1 103.8 %collective-permute-start.31 = (bf16[2,384,3,128]{1,3,2,0:T(8,128)(2,1)S(1)}, bf16[2,384,3,128]{1,3,2,0:T(8,128)(2,1)S(1)}, u32[]{:S(2)}, u32[]{:S(2)}) collective-permute-start(bf16[2,384,3,128]{1,3,2,0:T(8,128)(2,1)S(1)} %pad_maximum_fusion.12), channel_id=1, source_target_pairs={{12,0},{16,4},{20,8},{24,12},{28,16},{32,20},{36,24},{40,28},{44,3... | collective-permute-start | bytes 1769480 | tf_op jit(solution)/shard_map/ppermute | solution.py:24
  589.8 59.1 %collective-permute-start.32 = (bf16[2,384,3,128]{1,3,2,0:T(8,128)(2,1)S(1)}, bf16[2,384,3,128]{1,3,2,0:T(8,128)(2,1)S(1)}, u32[]{:S(2)}, u32[]{:S(2)}) collective-permute-start(bf16[2,384,3,128]{1,3,2,0:T(8,128)(2,1)S(1)} %pad_maximum_fusion.13), channel_id=1, source_target_pairs={{4,0},{8,4},{12,8},{16,12},{20,16},{24,20},{28,24},{32,28},{36,32}... | collective-permute-start | bytes 1769480 | tf_op jit(solution)/shard_map/ppermute | solution.py:24
  599.2 51.7 %collective-permute-start.33 = (bf16[2,384,3,128]{1,3,2,0:T(8,128)(2,1)S(1)}, bf16[2,384,3,128]{1,3,2,0:T(8,128)(2,1)S(1)}, u32[]{:S(2)}, u32[]{:S(2)}) collective-permute-start(bf16[2,384,3,128]{1,3,2,0:T(8,128)(2,1)S(1)} %pad_maximum_fusion.14), channel_id=1, source_target_pairs={{0,4},{4,8},{8,12},{12,16},{16,20},{20,24},{24,28},{28,32},{32,36}... | collective-permute-start | bytes 1769480 | tf_op jit(solution)/shard_map/ppermute | solution.py:24
  605.7 61.7 %collective-permute-start.34 = (bf16[2,384,3,128]{1,3,2,0:T(8,128)(2,1)S(1)}, bf16[2,384,3,128]{1,3,2,0:T(8,128)(2,1)S(1)}, u32[]{:S(2)}, u32[]{:S(2)}) collective-permute-start(bf16[2,384,3,128]{1,3,2,0:T(8,128)(2,1)S(1)} %pad_maximum_fusion.15), channel_id=1, source_target_pairs={{0,12},{4,16},{8,20},{12,24},{16,28},{20,32},{24,36},{28,40},{32,4... | collective-permute-start | bytes 1769480 | tf_op jit(solution)/shard_map/ppermute | solution.py:24
  644.1 72.4 %collective-permute-start.35 = (bf16[2,384,3,128]{1,3,2,0:T(8,128)(2,1)S(1)}, bf16[2,384,3,128]{1,3,2,0:T(8,128)(2,1)S(1)}, u32[]{:S(2)}, u32[]{:S(2)}) collective-permute-start(bf16[2,384,3,128]{1,3,2,0:T(8,128)(2,1)S(1)} %pad_maximum_fusion.16), channel_id=1, source_target_pairs={{0,16},{4,20},{8,24},{12,28},{16,32},{20,36},{24,40},{28,44},{32,4... | collective-permute-start | bytes 1769480 | tf_op jit(solution)/shard_map/ppermute | solution.py:24
  647.0 73.0 %collective-permute-start.36 = (bf16[2,384,3,128]{1,3,2,0:T(8,128)(2,1)S(1)}, bf16[2,384,3,128]{1,3,2,0:T(8,128)(2,1)S(1)}, u32[]{:S(2)}, u32[]{:S(2)}) collective-permute-start(bf16[2,384,3,128]{1,3,2,0:T(8,128)(2,1)S(1)} %pad_maximum_fusion.17), channel_id=1, source_target_pairs={{0,20},{4,24},{8,28},{12,32},{16,36},{20,40},{24,44},{28,48},{32,5... | collective-permute-start | bytes 1769480 | tf_op jit(solution)/shard_map/ppermute | solution.py:24
  648.9 73.0 %collective-permute-start.37 = (bf16[2,384,3,128]{1,3,2,0:T(8,128)(2,1)S(1)}, bf16[2,384,3,128]{1,3,2,0:T(8,128)(2,1)S(1)}, u32[]{:S(2)}, u32[]{:S(2)}) collective-permute-start(bf16[2,384,3,128]{1,3,2,0:T(8,128)(2,1)S(1)} %pad_maximum_fusion.18), channel_id=1, source_target_pairs={{0,12},{4,16},{8,20},{12,24},{16,28},{20,32},{24,36},{28,40},{32,4... | collective-permute-start | bytes 1769480 | tf_op jit(solution)/shard_map/ppermute | solution.py:24
  650.9 76.5 %collective-permute-start.38 = (bf16[2,384,3,128]{1,3,2,0:T(8,128)(2,1)S(1)}, bf16[2,384,3,128]{1,3,2,0:T(8,128)(2,1)S(1)}, u32[]{:S(2)}, u32[]{:S(2)}) collective-permute-start(bf16[2,384,3,128]{1,3,2,0:T(8,128)(2,1)S(1)} %pad_maximum_fusion.19), channel_id=1, source_target_pairs={{0,16},{4,20},{8,24},{12,28},{16,32},{20,36},{24,40},{28,44},{32,4... | collective-permute-start | bytes 1769480 | tf_op jit(solution)/shard_map/ppermute | solution.py:24
  667.4 61.2 %collective-permute-start.39 = (bf16[2,384,3,128]{1,3,2,0:T(8,128)(2,1)S(1)}, bf16[2,384,3,128]{1,3,2,0:T(8,128)(2,1)S(1)}, u32[]{:S(2)}, u32[]{:S(2)}) collective-permute-start(bf16[2,384,3,128]{1,3,2,0:T(8,128)(2,1)S(1)} %pad_maximum_fusion.20), channel_id=1, source_target_pairs={{0,20},{4,24},{8,28},{12,32},{16,36},{20,40},{24,44},{28,48},{32,5... | collective-permute-start | bytes 1769480 | tf_op jit(solution)/shard_map/ppermute | solution.py:24
  716.5 25.6 %collective-permute-start.40 = (bf16[2,384,3,128]{1,3,2,0:T(8,128)(2,1)S(1)}, bf16[2,384,3,128]{1,3,2,0:T(8,128)(2,1)S(1)}, u32[]{:S(2)}, u32[]{:S(2)}) collective-permute-start(bf16[2,384,3,128]{1,3,2,0:T(8,128)(2,1)S(1)} %pad_maximum_fusion.21), channel_id=1, source_target_pairs={{0,28},{4,32},{8,36},{12,40},{16,44},{20,48},{24,52},{28,56},{32,6... | collective-permute-start | bytes 1769480 | tf_op jit(solution)/shard_map/ppermute | solution.py:24
  720.0 66.0 %collective-permute-start.41 = (bf16[2,384,3,128]{1,3,2,0:T(8,128)(2,1)}, bf16[2,384,3,128]{1,3,2,0:T(8,128)(2,1)}, u32[]{:S(2)}, u32[]{:S(2)}) collective-permute-start(bf16[2,384,3,128]{1,3,2,0:T(8,128)(2,1)} %pad_maximum_fusion.22), channel_id=1, source_target_pairs={{0,32},{4,36},{8,40},{12,44},{16,48},{20,52},{24,56},{28,60},{32,6... | collective-permute-start | bytes 1769480 | tf_op jit(solution)/shard_map/ppermute | solution.py:24
  722.0 64.1 %collective-permute-start.42 = (bf16[2,384,3,128]{1,3,2,0:T(8,128)(2,1)}, bf16[2,384,3,128]{1,3,2,0:T(8,128)(2,1)}, u32[]{:S(2)}, u32[]{:S(2)}) collective-permute-start(bf16[2,384,3,128]{1,3,2,0:T(8,128)(2,1)} %pad_maximum_fusion.23), channel_id=1, source_target_pairs={{0,36},{4,40},{8,44},{12,48},{16,52},{20,56},{24,60},{28,64},{32,6... | collective-permute-start | bytes 1769480 | tf_op jit(solution)/shard_map/ppermute | solution.py:24
  727.4 58.7 %collective-permute-start.43 = (bf16[2,384,3,128]{1,3,2,0:T(8,128)(2,1)}, bf16[2,384,3,128]{1,3,2,0:T(8,128)(2,1)}, u32[]{:S(2)}, u32[]{:S(2)}) collective-permute-start(bf16[2,384,3,128]{1,3,2,0:T(8,128)(2,1)} %pad_maximum_fusion.24), channel_id=1, source_target_pairs={{0,44},{4,48},{8,52},{12,56},{16,60},{20,64},{24,68},{28,72},{32,7... | collective-permute-start | bytes 1769480 | tf_op jit(solution)/shard_map/ppermute | solution.py:24
  728.7 63.6 %collective-permute-start.44 = (bf16[2,384,3,128]{1,3,2,0:T(8,128)(2,1)}, bf16[2,384,3,128]{1,3,2,0:T(8,128)(2,1)}, u32[]{:S(2)}, u32[]{:S(2)}) collective-permute-start(bf16[2,384,3,128]{1,3,2,0:T(8,128)(2,1)} %pad_maximum_fusion.25), channel_id=1, source_target_pairs={{0,48},{4,52},{8,56},{12,60},{16,64},{20,68},{24,72},{28,76},{32,8... | collective-permute-start | bytes 1769480 | tf_op jit(solution)/shard_map/ppermute | solution.py:24
  742.9 63.9 %collective-permute-start.45 = (bf16[2,384,3,128]{1,3,2,0:T(8,128)(2,1)}, bf16[2,384,3,128]{1,3,2,0:T(8,128)(2,1)}, u32[]{:S(2)}, u32[]{:S(2)}) collective-permute-start(bf16[2,384,3,128]{1,3,2,0:T(8,128)(2,1)} %pad_maximum_fusion.26), channel_id=1, source_target_pairs={{0,52},{4,56},{8,60},{12,64},{16,68},{20,72},{24,76},{28,80},{32,8... | collective-permute-start | bytes 1769480 | tf_op jit(solution)/shard_map/ppermute | solution.py:24
  748.0 67.9 %all-to-all-start.5 = ((bf16[4,96,384]{2,1,0:T(8,128)(2,1)}), bf16[4,96,384]{2,1,0:T(8,128)(2,1)}, u32[]{:S(2)}, u32[]{:S(2)}) async-start(bf16[4,96,384]{2,1,0:T(8,128)(2,1)} %copy.1684), calls=%async_computation.5 | async-start | bytes 589824 | tf_op jit(solution)/shard_map/all_to_all | solution.py:163
  (125 other events, 3080.1 us)
where the time goes:
time: 860 us; the launch traced here: 846 us
  waiting for transfers between devices  404 us (47%)
  starting transfers between devices  234 us (27%)
  matrix products  144 us (17%)
  local copies, waits for them, and re-layouts  30.5 us (4%)
  between operations  20.6 us (2%)
  other arithmetic  13.9 us (2%)
    ppermute x46, waiting for transfers between devices, from_behind(): lax.ppermute(value, axis, [(source, source + steps) for source in range(l...  379 us
    ppermute x46, starting transfers between devices, from_behind(): lax.ppermute(value, axis, [(source, source + steps) for source in range(l...  173 us
    dot_general x27, matrix products, shards(): jnp.einsum('qhk,khd->qhd', weights.astype(jnp.bfloat16), value_cands[slot...  36.1 us
    all_to_all x1, starting transfers between devices, shards(): lax.all_to_all(flat_query, 'head', split_axis=0, concat_axis=1, tiled=True)  35.7 us
    dot_general x27, matrix products, key_terms(): jnp.einsum('qhk,qhd->khd', prob_low, grad_in, preferred_element_type=jnp....  35.2 us
    dot_general x21, matrix products, back_terms(): jnp.einsum('qhd,khd->qhk', grad_in, value_tile, preferred_element_type=jn...  24.6 us
  transfers between devices with their start and end apart: 54, of which 26 were waited for; matrix products, arithmetic and copies ran while one was open for 13% of the time, Pallas kernels for 0%

commit v1 on v0

v1 whole, which is shorter than its diff:
```python
import jax
import jax.numpy as jnp
from jax import lax
from jax.experimental import pallas as pl
from jax.experimental.pallas import tpu as pltpu
from jax.sharding import PartitionSpec as P

TILE = 384
HEADS = 12
HD = 128
QUARTER = 96
SLOTS = 18
EPSILON = 1e-06
SCALE = HD**-0.5
LOG2E = 1.4426950408889634
MESH = pl.DeviceIdType.MESH
VMEM_LIMIT = 50 * 1024 * 1024


def place():
    tm = lax.axis_index("tm")
    part = lax.axis_index("head")
    return tm, part


def worker_of(n, T, W, core):
    y = n % 4
    cc = n // 4
    x = 2 * T + cc // 2
    z = 2 * (cc % 2) + W
    return x * 8 + z * 2 + y // 2, (y % 2) * 2 + core


def work_here(tm, part):
    x = tm // 8
    z = tm // 2 % 4
    y = tm % 2 * 2 + part // 2
    cc = x % 2 * 2 + z // 2
    return cc < 3, cc * 4 + y, x // 2, z % 2, part % 2


def copy_to(src, dst, send_sem, recv_sem, device, tm, part, start):
    same = (device[0] == tm) & (device[1] == part)

    @pl.when(same)
    def _():
        if start:
            pltpu.make_async_copy(src, dst, recv_sem).start()

    @pl.when(jnp.logical_not(same))
    def _():
        copy = pltpu.make_async_remote_copy(
            src_ref=src, dst_ref=dst, send_sem=send_sem, recv_sem=recv_sem, device_id=device, device_id_type=MESH
        )
        if start:
            copy.start()
        else:
            copy.wait_send()


def arrived(ref, sem):
    pltpu.make_async_copy(ref, ref, sem).wait()


def gather_kernel(q_ref, k_ref, v_ref, g_ref, kv_ref, qg_ref, kv_stage, qg_stage, kv_send, qg_send, kv_recv, qg_recv):
    tm, part = place()
    t = tm // 8
    h = tm // 4 % 2
    w = tm % 4

    @pl.loop(0, HEADS)
    def _(n):
        lanes = pl.ds(pl.multiple_of(n * HD, HD), HD)
        k = k_ref[:, lanes].astype(jnp.float32)
        inverse = lax.rsqrt(jnp.mean(k * k, axis=-1, keepdims=True) + EPSILON)
        kv_stage[n, :, 0:HD] = (k * inverse).astype(jnp.bfloat16)
        kv_stage[n, :, HD:] = v_ref[:, lanes]
        qg_stage[n, :, 0:HD] = q_ref[:, lanes]
        qg_stage[n, :, HD:] = g_ref[:, lanes]

    rows = pl.ds(pl.multiple_of(part * QUARTER, QUARTER), QUARTER)

    def each(start):
        @pl.loop(0, HEADS)
        def _(n):
            tile = t % 2 * 2 + w % 2
            copy_to(
                qg_stage.at[n],
                qg_ref.at[tile, rows],
                qg_send.at[n],
                qg_recv.at[tile, part],
                worker_of(n, t // 2, w // 2, h),
                tm,
                part,
                start,
            )
            for T in range(2):
                for W in range(2):

                    @pl.when((t >= T) & (t < T + 3) & (w >= W) & (w < W + 3))
                    def _():
                        slot = ((t - T) * 2 + h) * 3 + (w - W)
                        for core in range(2):
                            copy_to(
                                kv_stage.at[n],
                                kv_ref.at[slot, rows],
                                kv_send.at[n, T * 2 + W, core],
                                kv_recv.at[slot, part],
                                worker_of(n, T, W, core),
                                tm,
                                part,
                                start,
                            )

    each(True)
    active = work_here(tm, part)[0]

    @pl.when(active)
    def _():
        for quarter in range(4):
            span = pl.ds(quarter * QUARTER, QUARTER)

            @pl.loop(0, 4)
            def _(tile):
                arrived(qg_ref.at[tile, span], qg_recv.at[tile, quarter])

            @pl.loop(0, SLOTS)
            def _(slot):
                arrived(kv_ref.at[slot, span], kv_recv.at[slot, quarter])

    each(False)


def nt(a, b):
    return lax.dot_general(a, b, (((1,), (1,)), ((), ())), preferred_element_type=jnp.float32)


def tn(a, b):
    return lax.dot_general(a, b, (((0,), (0,)), ((), ())), preferred_element_type=jnp.float32)


def attend_kernel(place_ref, window_ref, qg_ref, kv_ref, og_ref, dkv_ref, acc, dq_acc, dkv_acc, weights, ones, q_unit, scaled):
    @pl.when(place_ref[0] == 1)
    def _():
        T, W, core = place_ref[1], place_ref[2], place_ref[3]
        ones[...] = jnp.ones_like(ones)
        dkv_acc[...] = jnp.zeros_like(dkv_acc)

        @pl.loop(0, 4)
        def _(tile):
            ti = tile // 2
            wi = tile % 2
            s = (2 * T + ti) * 8 + core * 4 + 2 * W + wi

            def live(slot):
                dt = slot // 6 - T - ti
                dh = slot // 3 % 2 - core
                dw = slot % 3 - W - wi
                near = (dt >= -1) & (dt <= 1) & (dw >= -1) & (dw <= 1)
                at = jnp.where(near, 9 * (dt + 1) + 3 * (dh + 1) + dw + 1, 0)
                return near & (window_ref[s, at] == 1)

            q = qg_ref[tile, :, 0:HD].astype(jnp.float32)
            inverse = lax.rsqrt(jnp.mean(q * q, axis=-1, keepdims=True) + EPSILON)
            q_unit[...] = (q * inverse).astype(jnp.bfloat16)
            acc[...] = jnp.zeros_like(acc)
            dq_acc[...] = jnp.zeros_like(dq_acc)

            @pl.loop(0, SLOTS)
            def _(slot):
                @pl.when(live(slot))
                def _():
                    scores = nt(q_unit[...], kv_ref[slot, :, 0:HD])
                    low = jnp.exp2(scores * (SCALE * LOG2E)).astype(jnp.bfloat16)
                    weights[slot] = low
                    packed = jnp.concatenate([kv_ref[slot, :, HD:], ones[...]], axis=1)
                    acc[...] += jnp.dot(low, packed, preferred_element_type=jnp.float32)

            over = 1.0 / acc[:, HD:]
            out = (acc[:, 0:HD] * over).astype(jnp.bfloat16)
            og_ref[tile, :, 0:HD] = out
            grad = qg_ref[tile, :, HD:].astype(jnp.float32)
            row_dot = jnp.sum(grad * out.astype(jnp.float32), axis=-1, keepdims=True)
            scaled[:, 0:HD] = (q_unit[...].astype(jnp.float32) * (over * SCALE)).astype(jnp.bfloat16)
            scaled[:, HD:] = (grad * over).astype(jnp.bfloat16)

            @pl.loop(0, SLOTS)
            def _(slot):
                @pl.when(live(slot))
                def _():
                    low = weights[slot]
                    prob_grad = nt(qg_ref[tile, :, HD:], kv_ref[slot, :, HD:])
                    score_grad = (low.astype(jnp.float32) * (prob_grad - row_dot)).astype(jnp.bfloat16)
                    dq_acc[...] += jnp.dot(score_grad, kv_ref[slot, :, 0:HD], preferred_element_type=jnp.float32)
                    dkv_acc[slot, :, 0:HD] += tn(score_grad, scaled[:, 0:HD])
                    dkv_acc[slot, :, HD:] += tn(low, scaled[:, HD:])

            grad_in = dq_acc[...] * (over * SCALE)
            unit = q * inverse
            dq = inverse * (grad_in - unit * jnp.mean(grad_in * unit, axis=-1, keepdims=True))
            og_ref[tile, :, HD:] = dq.astype(jnp.bfloat16)

        @pl.loop(0, SLOTS)
        def _(slot):
            dkv_ref[slot] = dkv_acc[slot].astype(jnp.bfloat16)


def scatter_kernel(og_ref, dkv_ref, k_ref, o_ref, dq_ref, dk_ref, dv_ref, og_in, dkv_in, og_send, dkv_send, og_recv, dkv_recv):
    tm, part = place()
    t = tm // 8
    w = tm % 4
    active, n, T, W, core = work_here(tm, part)
    source = (T * 2 + W) * 2 + core

    def each(start):
        for quarter in range(4):
            span = pl.ds(quarter * QUARTER, QUARTER)

            @pl.loop(0, 4)
            def _(tile):
                owner = (2 * T + tile // 2) * 8 + core * 4 + 2 * W + tile % 2
                copy_to(
                    og_ref.at[tile, span],
                    og_in.at[n],
                    og_send.at[tile, quarter],
                    og_recv.at[n],
                    (owner, quarter),
                    tm,
                    part,
                    start,
                )

            @pl.loop(0, SLOTS)
            def _(slot):
                owner = (T + slot // 6) * 8 + slot // 3 % 2 * 4 + W + slot % 3
                copy_to(
                    dkv_ref.at[slot, span],
                    dkv_in.at[source, n],
                    dkv_send.at[slot, quarter],
                    dkv_recv.at[source, n],
                    (owner, quarter),
                    tm,
                    part,
                    start,
                )

    @pl.when(active)
    def _():
        each(True)

    def needed(T, W):
        return (t >= T) & (t < T + 3) & (w >= W) & (w < W + 3)

    @pl.loop(0, HEADS)
    def _(n):
        lanes = pl.ds(pl.multiple_of(n * HD, HD), HD)
        arrived(og_in.at[n], og_recv.at[n])
        o_ref[:, lanes] = og_in[n, :, 0:HD]
        dq_ref[:, lanes] = og_in[n, :, HD:]
        total = jnp.zeros((QUARTER, 2 * HD), jnp.float32)
        for T in range(2):
            for W in range(2):

                def take(total, T=T, W=W):
                    for core in range(2):
                        at = (T * 2 + W) * 2 + core
                        arrived(dkv_in.at[at, n], dkv_recv.at[at, n])
                        total = total + dkv_in[at, n].astype(jnp.float32)
                    return total

                total = lax.cond(needed(T, W), take, lambda total: total, total)
        k = k_ref[:, lanes].astype(jnp.float32)
        inverse = lax.rsqrt(jnp.mean(k * k, axis=-1, keepdims=True) + EPSILON)
        unit = k * inverse
        grad_in = total[:, 0:HD]
        dk = inverse * (grad_in - unit * jnp.mean(grad_in * unit, axis=-1, keepdims=True))
        dk_ref[:, lanes] = dk.astype(jnp.bfloat16)
        dv_ref[:, lanes] = total[:, HD:].astype(jnp.bfloat16)

    @pl.when(active)
    def _():
        each(False)


def shards(queries, keys, values, out_grad, window):
    low = jnp.bfloat16
    vmem = pl.BlockSpec(memory_space=pltpu.VMEM)
    smem = pl.BlockSpec(memory_space=pltpu.SMEM)
    hbm = pl.BlockSpec(memory_space=pl.ANY)
    dma = pltpu.SemaphoreType.DMA
    kv, qg = pl.pallas_call(
        gather_kernel,
        out_shape=(jax.ShapeDtypeStruct((SLOTS, TILE, 2 * HD), low), jax.ShapeDtypeStruct((4, TILE, 2 * HD), low)),
        in_specs=[vmem] * 4,
        out_specs=(hbm, hbm),
        scratch_shapes=[
            pltpu.VMEM((HEADS, QUARTER, 2 * HD), low),
            pltpu.VMEM((HEADS, QUARTER, 2 * HD), low),
            dma((HEADS, 4, 2)),
            dma((HEADS,)),
            dma((SLOTS, 4)),
            dma((4, 4)),
        ],
        compiler_params=pltpu.CompilerParams(has_side_effects=True, vmem_limit_bytes=VMEM_LIMIT),
        name="gather",
    )(queries, keys, values, out_grad)

    tm, part = place()
    active, _, T, W, core = work_here(tm, part)
    placed = jnp.stack([active.astype(jnp.int32), T, W, core])
    og, dkv = pl.pallas_call(
        attend_kernel,
        out_shape=(jax.ShapeDtypeStruct((4, TILE, 2 * HD), low), jax.ShapeDtypeStruct((SLOTS, TILE, 2 * HD), low)),
        in_specs=[smem, smem, vmem, vmem],
        out_specs=(vmem, vmem),
        scratch_shapes=[
            pltpu.VMEM((TILE, 2 * HD), jnp.float32),
            pltpu.VMEM((TILE, HD), jnp.float32),
            pltpu.VMEM((SLOTS, TILE, 2 * HD), jnp.float32),
            pltpu.VMEM((SLOTS, TILE, TILE), low),
            pltpu.VMEM((TILE, HD), low),
            pltpu.VMEM((TILE, HD), low),
            pltpu.VMEM((TILE, 2 * HD), low),
        ],
        compiler_params=pltpu.CompilerParams(vmem_limit_bytes=VMEM_LIMIT),
        name="attend",
    )(placed, window, qg, kv)

    return pl.pallas_call(
        scatter_kernel,
        out_shape=tuple(jax.ShapeDtypeStruct((QUARTER, HEADS * HD), low) for _ in range(4)),
        in_specs=[hbm, hbm, vmem],
        out_specs=(vmem,) * 4,
        scratch_shapes=[
            pltpu.VMEM((HEADS, QUARTER, 2 * HD), low),
            pltpu.VMEM((8, HEADS, QUARTER, 2 * HD), low),
            dma((4, 4)),
            dma((SLOTS, 4)),
            dma((HEADS,)),
            dma((8, HEADS)),
        ],
        compiler_params=pltpu.CompilerParams(has_side_effects=True, vmem_limit_bytes=VMEM_LIMIT),
        name="scatter",
    )(og, dkv, keys)


def solution(mesh):
    rows = P(("tm", "head"), None)
    return jax.shard_map(
        shards, mesh=mesh, in_specs=(rows, rows, rows, rows, P()), out_specs=(rows, rows, rows, rows), check_vma=False
    )
```

time: 860 us -> 314 us (0.37)
  the two profiles are of different devices: /device:TPU:100 before, /device:TPU:29 now
where the time goes in v1:
time: 314 us; the launch traced here: 311 us
  Pallas kernels  302 us (96%)
  local copies, waits for them, and re-layouts  7.42 us (2%)
    pallas_call x1, Pallas kernels, shards(): pl.pallas_call(scatter_kernel, out_shape=tuple((jax.ShapeDtypeStruct((QUA...  184 us
    pallas_call x1, Pallas kernels, shards(): pl.pallas_call(gather_kernel, out_shape=(jax.ShapeDtypeStruct((SLOTS, TIL...  85.2 us
    pallas_call x1, Pallas kernels, shards(): pl.pallas_call(attend_kernel, out_shape=(jax.ShapeDtypeStruct((4, TILE, 2...  32.9 us
    unnamed x16, local copies, waits for them, and re-layouts  7.42 us

profile of v1, /device:TPU:29, one launch (start us, length us, event | category | flops | bytes accessed | tf_op | source)
XLA Modules:
  0.0 310.5 jit_solution(9889987369860626520)
XLA Ops:
  0.7 0.1 pad_add_fusion.place_ref
  0.8 0.0 copy-start
  0.8 1.0 copy-done
  1.8 0.0 copy-start.2
  1.8 1.0 copy-done.2
  2.7 0.0 copy-start.3
  2.7 1.0 copy-done.3
  3.7 0.0 copy-start.4
  3.7 1.0 copy-done.4
  4.7 0.0 copy-start.1
  4.7 85.2 %gather.1 = (bf16[18,384,256]{2,1,0:T(8,128)(2,1)}, bf16[4,384,256]{2,1,0:T(8,128)(2,1)S(1)}) custom-call(bf16[96,1536]{1,0:T(8,128)(2,1)S(1)} %copy-done.2, bf16[96,1536]{1,0:T(8,128)(2,1)S(1)} %copy-done, bf16[96,1536]{1,0:T(8,128)(2,1)S(1)} %copy-done.3, bf16[96,1536]{1,0:T(8,128)(2,1)S(1)} %copy-done.4), custom_call_target="tpu_custom_call" | custom-call | tf_op jit(solution)/shard_map/gather/pallas_call | solution.py:291
  89.9 0.0 copy-start.5
  89.9 0.7 copy-done.5
  90.6 32.9 %attend.1 = (bf16[4,384,256]{2,1,0:T(8,128)(2,1)S(1)}, bf16[18,384,256]{2,1,0:T(8,128)(2,1)}) custom-call(s32[4]{0:T(128)S(1)} %pad_add_fusion.place_ref, s32[32,27]{1,0:T(8,128)S(1)} %copy-done.5, bf16[4,384,256]{2,1,0:T(8,128)(2,1)S(1)} %get-tuple-element.8.qg_ref, bf16[18,384,256]{2,1,0:T(8,128)(2,1)} %get-tuple-element.9.kv_ref), custom_call_target="tpu_custom_call" | custom-call | tf_op jit(solution)/shard_map/attend/pallas_call | solution.py:311
  123.5 0.0 copy-done.1
  123.5 184.1 %scatter.1 = (bf16[96,1536]{1,0:T(8,128)(2,1)S(1)}, bf16[96,1536]{1,0:T(8,128)(2,1)S(1)}, bf16[96,1536]{1,0:T(8,128)(2,1)S(1)}, bf16[96,1536]{1,0:T(8,128)(2,1)S(1)}) custom-call(bf16[4,384,256]{2,1,0:T(8,128)(2,1)S(1)} %get-tuple-element.10.og_ref, bf16[18,384,256]{2,1,0:T(8,128)(2,1)} %get-tuple-element.11.dkv_ref, bf16[96,1536]{1,0:T(8,128)(2,1)S(1)} %copy-done.1), custom_call_target="tpu_custom_call" | custom-call | tf_op jit(solution)/shard_map/scatter/pallas_call | solution.py:329
  307.6 0.7 copy.13
  308.4 0.7 copy.14
  309.1 0.7 copy.15
  309.8 0.7 copy.16
Async XLA Ops:
  0.8 1.0 copy-start
  1.8 1.0 copy-start.2
  2.7 1.0 copy-start.3
  3.7 1.0 copy-start.4
  4.7 118.8 %copy-start.1 = (bf16[96,1536]{1,0:T(8,128)(2,1)S(1)}, bf16[96,1536]{1,0:T(8,128)(2,1)}, u32[]{:S(2)}) copy-start(bf16[96,1536]{1,0:T(8,128)(2,1)} %k_ref.3) | copy-start | bytes 884740
  89.9 0.7 copy-start.5

commit v2 on v0

v2 whole, which is shorter than its diff:
```python
import jax
import jax.numpy as jnp
from jax import lax
from jax.experimental import pallas as pl
from jax.experimental.pallas import tpu as pltpu
from jax.sharding import PartitionSpec as P

TILE = 384
HEADS = 12
HD = 128
QUARTER = 96
SLOTS = 18
EPSILON = 1e-06
SCALE = HD**-0.5
LOG2E = 1.4426950408889634
MESH = pl.DeviceIdType.MESH
VMEM_LIMIT = 60 * 1024 * 1024
LOW = jnp.bfloat16

QUERY_AT = ((0, 1), (0, 0), (1, 0), (1, 1))
KINDS = ((0, 8, 0, 4), (8, 4, 0, 2), (12, 4, 1, 2), (16, 2, 1, 1))
CHIPS = (
    (0, 9, 11, 12, 22, 28, 30, 36, 38, 42, 49, 59),
    (3, 4, 13, 15, 17, 26, 35, 40, 41, 47, 48, 61),
    (6, 7, 19, 25, 27, 34, 44, 45, 51, 54, 57, 62),
    (2, 8, 16, 20, 21, 31, 33, 39, 53, 55, 58, 60),
)


def pick(table, index):
    found = jnp.int32(table[0])
    for at in range(1, len(table)):
        found = jnp.where(index == at, jnp.int32(table[at]), found)
    return found


def worker_of(n, block, core):
    chip = pick(CHIPS[block], n)
    x, y, z = chip // 16, chip // 4 % 4, chip % 4
    return x * 8 + z * 2 + y // 2, (y % 2) * 2 + core


def work_here(tm, part):
    x, y, z = tm // 8, tm % 2 * 2 + part // 2, tm // 2 % 4
    chip = x * 16 + y * 4 + z
    code = jnp.int32(-1)
    for block in range(4):
        for n in range(HEADS):
            code = jnp.where(chip == CHIPS[block][n], jnp.int32(block * HEADS + n), code)
    active = code >= 0
    code = jnp.where(active, code, 0)
    block = code // HEADS
    return active, code % HEADS, block // 2, block % 2, part % 2


def absolute(half, near):
    return 1 + half + near * (2 * half - 1)


def relative(half, index):
    return (index - 1 - half) * (2 * half - 1)


def slot_at(kind, i):
    if kind == 0:
        return i // 4, i % 2, i // 2 % 2
    if kind == 1:
        return -1, i % 2, i // 2
    if kind == 2:
        return i // 2, i % 2, -1
    return -1, i % 2, -1


def slot_number(near_t, h, near_w):
    return jnp.where(
        near_t >= 0,
        jnp.where(near_w >= 0, (near_t * 2 + near_w) * 2 + h, 12 + near_t * 2 + h),
        jnp.where(near_w >= 0, 8 + near_w * 2 + h, 16 + h),
    )


def query_number(near_t, near_w):
    return jnp.where(near_t == 0, 1 - near_w, 2 + near_w)


def copy_to(src, dst, send_sem, recv_sem, device, here, start):
    same = (device[0] == here[0]) & (device[1] == here[1])

    @pl.when(same)
    def _():
        if start:
            pltpu.make_async_copy(src, dst, recv_sem).start()

    @pl.when(jnp.logical_not(same))
    def _():
        copy = pltpu.make_async_remote_copy(
            src_ref=src, dst_ref=dst, send_sem=send_sem, recv_sem=recv_sem, device_id=device, device_id_type=MESH
        )
        if start:
            copy.start()
        else:
            copy.wait_send()


def arrived(ref, sem):
    pltpu.make_async_copy(ref, ref, sem).wait()


def nt(a, b):
    return lax.dot_general(a, b, (((1,), (1,)), ((), ())), preferred_element_type=jnp.float32)


def tn(a, b):
    return lax.dot_general(a, b, (((0,), (0,)), ((), ())), preferred_element_type=jnp.float32)


def quarter(j):
    return pl.ds(pl.multiple_of(j * QUARTER, QUARTER), QUARTER)


def lanes_of(n):
    return pl.ds(pl.multiple_of(n * HD, HD), HD)


def thrice(value):
    return jnp.concatenate([value] * 3, axis=1)


def fused_kernel(
    window_ref,
    q_ref,
    k_ref,
    v_ref,
    g_ref,
    o_ref,
    dq_ref,
    dk_ref,
    dv_ref,
    kv_stage,
    qg_stage,
    kv,
    qg,
    q_unit,
    weights0,
    weights1,
    weights2,
    weights3,
    acc,
    dq_acc,
    over,
    row_dot,
    scaled,
    o_stage,
    dq_stage,
    part_sum,
    sib_send,
    sib_recv,
    sum_stage,
    dkv_in,
    kv_send,
    qg_send,
    kv_recv,
    qg_recv,
    relay_send,
    sib_sent,
    sib_got,
    o_send,
    dq_send,
    sum_send,
    o_recv,
    dq_recv,
    dkv_recv,
):
    tm, part = lax.axis_index("tm"), lax.axis_index("head")
    here = (tm, part)
    t, h, w = tm // 8, tm // 4 % 2, tm % 4
    active, head, T, W, core = work_here(tm, part)
    block = T * 2 + W
    sibling = (tm, part + 1 - 2 * core)
    weights = (weights0, weights1, weights2, weights3)

    @pl.loop(0, HEADS)
    def _(n):
        lanes = lanes_of(n)
        k = k_ref[:, lanes].astype(jnp.float32)
        inverse = lax.rsqrt(jnp.mean(k * k, axis=-1, keepdims=True) + EPSILON)
        kv_stage[n, :, 0:HD] = (k * inverse).astype(LOW)
        kv_stage[n, :, HD:] = v_ref[:, lanes]
        qg_stage[n, :, 0:HD] = q_ref[:, lanes]
        qg_stage[n, :, HD:] = g_ref[:, lanes]

    def send_queries(start):
        for b in range(4):

            @pl.when((t // 2 == b // 2) & (w // 2 == b % 2))
            def _():
                at = query_number(relative(b // 2, t), relative(b % 2, w))

                @pl.loop(0, HEADS)
                def _(n):
                    copy_to(
                        qg_stage.at[n],
                        qg.at[at, quarter(part)],
                        qg_send.at[n],
                        qg_recv.at[at, part],
                        worker_of(n, b, h),
                        here,
                        start,
                    )

    def send_keys(own, start):
        for b in range(4):
            near_t, near_w = relative(b // 2, t), relative(b % 2, w)
            inside = (near_t >= 0) & (near_w >= 0)
            reached = (near_t <= 1) & (near_w <= 1) & (near_t >= -1) & (near_w >= -1)

            @pl.when(inside if own else reached & jnp.logical_not(inside))
            def _():
                slot = slot_number(near_t, h, near_w)

                @pl.loop(0, HEADS)
                def _(n):
                    copy_to(
                        kv_stage.at[n],
                        kv.at[slot, quarter(part)],
                        kv_send.at[n, b],
                        kv_recv.at[slot, part],
                        worker_of(n, b, core),
                        here,
                        start,
                    )

    send_queries(True)
    send_keys(True, True)
    send_keys(False, True)

    def relay(slot, start):
        for y in range(2):
            j = 2 * y + core
            if start:
                arrived(kv.at[slot, quarter(j)], kv_recv.at[slot, j])
            copy = pltpu.make_async_remote_copy(
                src_ref=kv.at[slot, quarter(j)],
                dst_ref=kv.at[slot, quarter(j)],
                send_sem=relay_send.at[slot, y],
                recv_sem=kv_recv.at[slot, j],
                device_id=sibling,
                device_id_type=MESH,
            )
            if start:
                copy.start()
            else:
                copy.wait_send()

    def relayed(slot):
        for y in range(2):
            j = 2 * y + 1 - core
            arrived(kv.at[slot, quarter(j)], kv_recv.at[slot, j])

    def score_step(kind, i):
        first, count, q0, qn = KINDS[kind]
        slot = first + i
        near_t, kh, near_w = slot_at(kind, i)

        @pl.when(slot + 1 < SLOTS)
        def _():
            relay(slot + 1, True)

        relayed(slot)
        scores = nt(q_unit[q0 * TILE : (q0 + qn) * TILE], kv[slot, :, 0:HD])
        lows = []
        for u in range(qn):
            qt, qw = QUERY_AT[q0 + u]
            dt = absolute(T, near_t) - absolute(T, qt)
            dw = absolute(W, near_w) - absolute(W, qw)
            tile = absolute(T, qt) * 8 + core * 4 + absolute(W, qw)
            live = window_ref[tile, 9 * (dt + 1) + 3 * (kh - core + 1) + dw + 1]
            bias = (live.astype(jnp.float32) - 1.0) * 1e30
            weight = jnp.exp2(scores[u * TILE : (u + 1) * TILE] * (SCALE * LOG2E) + bias)
            rows = slice((q0 + u) * TILE, (q0 + u + 1) * TILE)
            acc[rows, HD:] += weight[:, 0:HD] + weight[:, HD : 2 * HD] + weight[:, 2 * HD :]
            lows.append(weight.astype(LOW))
        low = jnp.concatenate(lows, axis=0) if qn > 1 else lows[0]
        weights[kind][i] = low
        acc[q0 * TILE : (q0 + qn) * TILE, 0:HD] += jnp.dot(low, kv[slot, :, HD:], preferred_element_type=jnp.float32)

    def send_sum(slot, coords, start):
        near_t, kh, near_w = coords
        owner = absolute(T, near_t) * 8 + kh * 4 + absolute(W, near_w)
        for y in range(2):
            copy_to(
                sum_stage.at[slot, y],
                dkv_in.at[block, head],
                sum_send.at[slot, y],
                dkv_recv.at[block, head],
                (owner, 2 * y + core),
                here,
                start,
            )

    def to_sibling(slot):
        return pltpu.make_async_remote_copy(
            src_ref=sib_send.at[slot],
            dst_ref=sib_recv.at[slot],
            send_sem=sib_sent.at[slot],
            recv_sem=sib_got.at[slot],
            device_id=sibling,
            device_id_type=MESH,
        )

    def finish_sum(slot, coords):
        to_sibling(slot).wait_recv()
        for y in range(2):
            mine = part_sum[slot % 2, quarter(2 * y + core)]
            sum_stage[slot, y] = (mine + sib_recv[slot, y].astype(jnp.float32)).astype(LOW)
        send_sum(slot, coords, True)

    def grad_step(kind, i):
        first, count, q0, qn = KINDS[kind]
        slot = first + i
        rows = slice(q0 * TILE, (q0 + qn) * TILE)
        low = weights[kind][i]
        prob_grad = nt(scaled[rows, 2 * HD :], kv[slot, :, HD:])
        score_grad = (low.astype(jnp.float32) * (prob_grad - thrice(row_dot[rows]))).astype(LOW)
        dq_acc[rows] += jnp.dot(score_grad, kv[slot, :, 0:HD], preferred_element_type=jnp.float32)
        part_sum[slot % 2, :, 0:HD] = tn(score_grad, scaled[rows, 0:HD])
        part_sum[slot % 2, :, HD:] = tn(low, scaled[rows, HD : 2 * HD])
        for y in range(2):
            sib_send[slot, y] = part_sum[slot % 2, quarter(2 * y + 1 - core)].astype(LOW)
        to_sibling(slot).start()

    def query_owner(u):
        qt, qw = QUERY_AT[u]
        return absolute(T, qt) * 8 + core * 4 + absolute(W, qw)

    def send_result(stage, dst, send_sem, recv_sem, start):
        for u in range(4):
            for j in range(4):
                copy_to(
                    stage.at[u, quarter(j)],
                    dst.at[:, lanes_of(head)],
                    send_sem.at[u, j],
                    recv_sem.at[head],
                    (query_owner(u), j),
                    here,
                    start,
                )

    @pl.when(active)
    def _():
        for u in range(4):
            for j in range(4):
                arrived(qg.at[u, quarter(j)], qg_recv.at[u, j])
            q = qg[u, :, 0:HD].astype(jnp.float32)
            inverse = lax.rsqrt(jnp.mean(q * q, axis=-1, keepdims=True) + EPSILON)
            rows = slice(u * TILE, (u + 1) * TILE)
            q_unit[rows] = (q * inverse).astype(LOW)
            scaled[rows, 2 * HD :] = qg[u, :, HD:]
        acc[...] = jnp.zeros_like(acc)
        dq_acc[...] = jnp.zeros_like(dq_acc)
        relay(0, True)
        for kind in range(4):

            @pl.loop(0, KINDS[kind][1])
            def _(i):
                score_step(kind, i)

        for u in range(4):
            rows = slice(u * TILE, (u + 1) * TILE)
            over[rows] = jnp.broadcast_to(1.0 / jnp.sum(acc[rows, HD:], axis=-1, keepdims=True), (TILE, HD))
            out = (acc[rows, 0:HD] * over[rows]).astype(LOW)
            o_stage[u] = out
            grad = qg[u, :, HD:].astype(jnp.float32)
            dot = jnp.sum(grad * out.astype(jnp.float32), axis=-1, keepdims=True)
            row_dot[rows] = jnp.broadcast_to(dot, (TILE, HD))
            scaled[rows, 0:HD] = (q_unit[rows].astype(jnp.float32) * (over[rows] * SCALE)).astype(LOW)
            scaled[rows, HD : 2 * HD] = (grad * over[rows]).astype(LOW)
        send_result(o_stage, o_ref, o_send, o_recv, True)

        for kind in (3, 2, 1, 0):

            @pl.loop(0, KINDS[kind][1])
            def _(i):
                grad_step(kind, i)

                @pl.when(i > 0)
                def _():
                    finish_sum(KINDS[kind][0] + i - 1, slot_at(kind, i - 1))

            last = KINDS[kind][1] - 1
            finish_sum(KINDS[kind][0] + last, slot_at(kind, last))

        for u in range(4):
            rows = slice(u * TILE, (u + 1) * TILE)
            q = qg[u, :, 0:HD].astype(jnp.float32)
            inverse = lax.rsqrt(jnp.mean(q * q, axis=-1, keepdims=True) + EPSILON)
            unit = q * inverse
            grad_in = dq_acc[rows] * (over[rows] * SCALE)
            dq = inverse * (grad_in - unit * jnp.mean(grad_in * unit, axis=-1, keepdims=True))
            dq_stage[u] = dq.astype(LOW)
        send_result(dq_stage, dq_ref, dq_send, dq_recv, True)

    def reached(b):
        near_t, near_w = relative(b // 2, t), relative(b % 2, w)
        return (near_t <= 1) & (near_w <= 1) & (near_t >= -1) & (near_w >= -1)

    @pl.loop(0, HEADS)
    def _(n):
        lanes = lanes_of(n)
        total = jnp.zeros((QUARTER, 2 * HD), jnp.float32)
        for b in range(4):

            def take(total, b=b):
                arrived(dkv_in.at[b, n], dkv_recv.at[b, n])
                return total + dkv_in[b, n].astype(jnp.float32)

            total = lax.cond(reached(b), take, lambda total: total, total)
        k = k_ref[:, lanes].astype(jnp.float32)
        inverse = lax.rsqrt(jnp.mean(k * k, axis=-1, keepdims=True) + EPSILON)
        unit = k * inverse
        grad_in = total[:, 0:HD]
        dk = inverse * (grad_in - unit * jnp.mean(grad_in * unit, axis=-1, keepdims=True))
        dk_ref[:, lanes] = dk.astype(LOW)
        dv_ref[:, lanes] = total[:, HD:].astype(LOW)

    @pl.loop(0, HEADS)
    def _(n):
        arrived(o_ref.at[:, lanes_of(n)], o_recv.at[n])
        arrived(dq_ref.at[:, lanes_of(n)], dq_recv.at[n])

    send_queries(False)
    send_keys(True, False)
    send_keys(False, False)

    @pl.when(active)
    def _():
        @pl.loop(0, SLOTS)
        def _(slot):
            relay(slot, False)
            to_sibling(slot).wait_send()

        for kind in range(4):

            @pl.loop(0, KINDS[kind][1])
            def _(i):
                send_sum(KINDS[kind][0] + i, slot_at(kind, i), False)

        send_result(o_stage, o_ref, o_send, o_recv, False)
        send_result(dq_stage, dq_ref, dq_send, dq_recv, False)


def shards(queries, keys, values, out_grad, window):
    vmem = pl.BlockSpec(memory_space=pltpu.VMEM)
    smem = pl.BlockSpec(memory_space=pltpu.SMEM)
    dma = pltpu.SemaphoreType.DMA
    f32 = jnp.float32
    return pl.pallas_call(
        fused_kernel,
        out_shape=tuple(jax.ShapeDtypeStruct((QUARTER, HEADS * HD), LOW) for _ in range(4)),
        in_specs=[smem] + [vmem] * 4,
        out_specs=(vmem,) * 4,
        scratch_shapes=[
            pltpu.VMEM((HEADS, QUARTER, 2 * HD), LOW),
            pltpu.VMEM((HEADS, QUARTER, 2 * HD), LOW),
            pltpu.VMEM((SLOTS, TILE, 2 * HD), LOW),
            pltpu.VMEM((4, TILE, 2 * HD), LOW),
            pltpu.VMEM((4 * TILE, HD), LOW),
            pltpu.VMEM((8, 4 * TILE, TILE), LOW),
            pltpu.VMEM((4, 2 * TILE, TILE), LOW),
            pltpu.VMEM((4, 2 * TILE, TILE), LOW),
            pltpu.VMEM((2, TILE, TILE), LOW),
            pltpu.VMEM((4 * TILE, 2 * HD), f32),
            pltpu.VMEM((4 * TILE, HD), f32),
            pltpu.VMEM((4 * TILE, HD), f32),
            pltpu.VMEM((4 * TILE, HD), f32),
            pltpu.VMEM((4 * TILE, 3 * HD), LOW),
            pltpu.VMEM((4, TILE, HD), LOW),
            pltpu.VMEM((4, TILE, HD), LOW),
            pltpu.VMEM((2, TILE, 2 * HD), f32),
            pltpu.VMEM((SLOTS, 2, QUARTER, 2 * HD), LOW),
            pltpu.VMEM((SLOTS, 2, QUARTER, 2 * HD), LOW),
            pltpu.VMEM((SLOTS, 2, QUARTER, 2 * HD), LOW),
            pltpu.VMEM((4, HEADS, QUARTER, 2 * HD), LOW),
            dma((HEADS, 4)),
            dma((HEADS,)),
            dma((SLOTS, 4)),
            dma((4, 4)),
            dma((SLOTS, 2)),
            dma((SLOTS,)),
            dma((SLOTS,)),
            dma((4, 4)),
            dma((4, 4)),
            dma((SLOTS, 2)),
            dma((HEADS,)),
            dma((HEADS,)),
            dma((4, HEADS)),
        ],
        compiler_params=pltpu.CompilerParams(has_side_effects=True, vmem_limit_bytes=VMEM_LIMIT),
        name="attend",
    )(window, queries, keys, values, out_grad)


def solution(mesh):
    rows = P(("tm", "head"), None)
    return jax.shard_map(
        shards, mesh=mesh, in_specs=(rows, rows, rows, rows, P()), out_specs=(rows, rows, rows, rows), check_vma=False
    )
```

time: 860 us -> 118 us (0.14)
  the two profiles are of different devices: /device:TPU:100 before, /device:TPU:29 now
where the time goes in v2:
time: 118 us
  Pallas kernels  113 us (96%)
  local copies, waits for them, and re-layouts  4.59 us (4%)
    pallas_call x1, Pallas kernels, shards(): pl.pallas_call(fused_kernel, out_shape=tuple((jax.ShapeDtypeStruct((QUART...  113 us
    unnamed x10, local copies, waits for them, and re-layouts  4.59 us

profile of v2, /device:TPU:29, one launch (start us, length us, event | category | flops | bytes accessed | tf_op | source)
XLA Modules:
  0.0 117.8 jit_solution(18293136732418669596)
XLA Ops:
  0.6 112.5 %attend.1 = (bf16[96,1536]{1,0:T(8,128)(2,1)}, bf16[96,1536]{1,0:T(8,128)(2,1)}, bf16[96,1536]{1,0:T(8,128)(2,1)}, bf16[96,1536]{1,0:T(8,128)(2,1)}) custom-call(s32[32,27]{1,0:T(8,128)} %window_ref.1, bf16[96,1536]{1,0:T(8,128)(2,1)} %q_ref.1, bf16[96,1536]{1,0:T(8,128)(2,1)} %k_ref.1, bf16[96,1536]{1,0:T(8,128)(2,1)} %v_ref.1, bf16[96,1536]{1,0:T(8,128)(2,1)} %g_ref.1), custom_call_target="tpu_custom_call" | custom-call | tf_op jit(solution)/shard_map/attend/pallas_call | solution.py:457
  113.2 0.0 copy-start.2
  113.2 1.7 %copy.13 = bf16[96,1536]{1,0:T(8,128)(2,1)} copy(bf16[96,1536]{1,0:T(8,128)(2,1)} %get-tuple-element.8) | data formatting | bytes 589824
  114.9 0.0 copy-done.2
  114.9 0.0 copy-start.1
  114.9 0.7 copy.14
  115.6 0.4 copy-done.1
  116.0 0.0 copy-start
  116.0 0.7 copy.15
  116.7 0.4 copy-done
  117.1 0.7 copy.16
Async XLA Ops:
  113.2 1.8 %copy-start.2 = (bf16[96,1536]{1,0:T(8,128)(2,1)S(1)}, bf16[96,1536]{1,0:T(8,128)(2,1)}, u32[]{:S(2)}) copy-start(bf16[96,1536]{1,0:T(8,128)(2,1)} %get-tuple-element.9) | copy-start | bytes 884740
  114.9 1.1 copy-start.1
  116.0 1.1 copy-start

commit v3 on v2

v3 whole, which is shorter than its diff:
```python
import jax
import jax.numpy as jnp
from jax import lax
from jax.experimental import pallas as pl
from jax.experimental.pallas import tpu as pltpu
from jax.sharding import PartitionSpec as P

TILE = 384
HEADS = 12
HD = 128
QUARTER = 96
SLOTS = 18
EPSILON = 1e-06
SCALE = HD**-0.5
LOG2E = 1.4426950408889634
MESH = pl.DeviceIdType.MESH
VMEM_LIMIT = 60 * 1024 * 1024
LOW = jnp.bfloat16

QUERY_AT = ((0, 1), (0, 0), (1, 0), (1, 1))
KINDS = ((0, 8, 0, 4), (8, 4, 0, 2), (12, 4, 1, 2), (16, 2, 1, 1))
CHIPS = (
    (16, 6, 24, 14, 18, 4, 26, 12, 0, 22, 8, 30),
    (17, 7, 25, 15, 19, 5, 23, 13, 1, 27, 9, 31),
    (32, 54, 40, 62, 34, 52, 42, 60, 48, 38, 56, 46),
    (33, 55, 41, 63, 35, 53, 39, 61, 49, 43, 57, 47),
)


def pick(table, index):
    found = jnp.int32(table[0])
    for at in range(1, len(table)):
        found = jnp.where(index == at, jnp.int32(table[at]), found)
    return found


def worker_of(n, block, core):
    chip = pick(sum(CHIPS, ()), block * HEADS + n)
    x, y, z = chip // 16, chip // 4 % 4, chip % 4
    return x * 8 + z * 2 + y // 2, (y % 2) * 2 + core


def work_here(tm, part):
    x, y, z = tm // 8, tm % 2 * 2 + part // 2, tm // 2 % 4
    chip = x * 16 + y * 4 + z
    code = jnp.int32(-1)
    for at, worker in enumerate(sum(CHIPS, ())):
        code = jnp.where(chip == worker, jnp.int32(at), code)
    active = code >= 0
    code = jnp.where(active, code, 0)
    return active, code % HEADS, code // HEADS, part % 2


def absolute(half, near):
    return 1 + half + near * (2 * half - 1)


def relative(half, index):
    return (index - 1 - half) * (2 * half - 1)


def slot_at(kind, i):
    if kind == 0:
        return i // 4, i % 2, i // 2 % 2
    if kind == 1:
        return -1, i % 2, i // 2
    if kind == 2:
        return i // 2, i % 2, -1
    return -1, i % 2, -1


def slot_number(near_t, h, near_w):
    return jnp.where(
        near_t >= 0,
        jnp.where(near_w >= 0, (near_t * 2 + near_w) * 2 + h, 12 + near_t * 2 + h),
        jnp.where(near_w >= 0, 8 + near_w * 2 + h, 16 + h),
    )


def query_number(near_t, near_w):
    return jnp.where(near_t == 0, 1 - near_w, 2 + near_w)


def copy_to(src, dst, send_sem, recv_sem, device, here, start):
    same = (device[0] == here[0]) & (device[1] == here[1])

    @pl.when(same)
    def _():
        if start:
            pltpu.make_async_copy(src, dst, recv_sem).start()

    @pl.when(jnp.logical_not(same))
    def _():
        copy = pltpu.make_async_remote_copy(
            src_ref=src, dst_ref=dst, send_sem=send_sem, recv_sem=recv_sem, device_id=device, device_id_type=MESH
        )
        if start:
            copy.start()
        else:
            copy.wait_send()


def arrived(ref, sem):
    pltpu.make_async_copy(ref, ref, sem).wait()


def nt(a, b):
    return lax.dot_general(a, b, (((1,), (1,)), ((), ())), preferred_element_type=jnp.float32)


def tn(a, b):
    return lax.dot_general(a, b, (((0,), (0,)), ((), ())), preferred_element_type=jnp.float32)


def quarter(j):
    return pl.ds(pl.multiple_of(j * QUARTER, QUARTER), QUARTER)


def lanes_of(n):
    return pl.ds(pl.multiple_of(n * HD, HD), HD)


def thrice(value):
    return jnp.concatenate([value] * 3, axis=1)


def attend_kernel(
    window_ref,
    q_hbm,
    k_hbm,
    v_hbm,
    g_hbm,
    o_ref,
    dq_ref,
    dkv_ref,
    q_in,
    k_in,
    v_in,
    g_in,
    kv_stage,
    qg_stage,
    kv,
    qg,
    q_unit,
    weights0,
    weights1,
    weights2,
    weights3,
    acc,
    dq_acc,
    over,
    row_dot,
    scaled,
    o_stage,
    dq_stage,
    part_sum,
    sib_send,
    sib_recv,
    sum_stage,
    near_recv,
    in_sem,
    kv_send,
    qg_send,
    kv_recv,
    qg_recv,
    relay_send,
    time_send,
    wide_send,
    sib_sent,
    sib_got,
    near_got,
    o_send,
    dq_send,
    sum_send,
    o_recv,
    dq_recv,
    dkv_recv,
):
    tm, part = lax.axis_index("tm"), lax.axis_index("head")
    here = (tm, part)
    t, h, w = tm // 8, tm // 4 % 2, tm % 4
    home = t // 2 * 2 + w // 2
    active, head, block, core = work_here(tm, part)
    T, W = block // 2, block % 2
    sibling = (tm, part + 1 - 2 * core)
    time_near = worker_of(head, (1 - T) * 2 + W, core)
    wide_near = worker_of(head, T * 2 + 1 - W, core)
    weights = (weights0, weights1, weights2, weights3)

    def copy_in(i):
        return pltpu.make_async_copy((k_hbm, v_hbm, q_hbm, g_hbm)[i], (k_in, v_in, q_in, g_in)[i], in_sem.at[i])

    for i in range(4):
        copy_in(i).start()

    def tile_of(near_t, kh, near_w):
        return absolute(T, near_t) * 8 + kh * 4 + absolute(W, near_w)

    barrier = pltpu.get_barrier_semaphore()

    def greet(device, count):
        other = jnp.logical_not((device[0] == tm) & (device[1] == part))

        @pl.when(other)
        def _():
            pl.semaphore_signal(barrier, inc=1, device_id=device, device_id_type=MESH)

        return count + other.astype(jnp.int32)

    def greet_workers(n, count):
        count = greet(worker_of(n, home, core), count)
        return lax.cond(h != core, lambda c: greet(worker_of(n, home, h), c), lambda c: c, count)

    greeted = lax.fori_loop(0, HEADS, greet_workers, jnp.int32(0))

    def greet_owners(i, count):
        owner = tile_of(*slot_at(0, i))
        for y in range(2):
            count = greet((owner, 2 * y + core), count)

        def others(count):
            for y in range(2):
                count = greet((owner, 2 * y + 1 - core), count)
            return count

        return lax.cond(i % 2 == core, others, lambda count: count, count)

    def greet_all(count):
        count = lax.fori_loop(0, 8, greet_owners, count)
        for device in (sibling, time_near, wide_near):
            count = greet(device, count)
        return count

    greeted = lax.cond(active, greet_all, lambda count: count, greeted)

    copy_in(0).wait()
    copy_in(1).wait()

    @pl.loop(0, HEADS)
    def _(n):
        lanes = lanes_of(n)
        k = k_in[:, lanes].astype(jnp.float32)
        inverse = lax.rsqrt(jnp.mean(k * k, axis=-1, keepdims=True) + EPSILON)
        kv_stage[n, :, 0:HD] = (k * inverse).astype(LOW)
        kv_stage[n, :, HD:] = v_in[:, lanes]

    copy_in(2).wait()
    copy_in(3).wait()

    @pl.loop(0, HEADS)
    def _(n):
        lanes = lanes_of(n)
        qg_stage[n, :, 0:HD] = q_in[:, lanes]
        qg_stage[n, :, HD:] = g_in[:, lanes]

    pl.semaphore_wait(barrier, greeted)
    near_t, near_w = relative(t // 2, t), relative(w // 2, w)

    def send_keys(start):
        slot = slot_number(near_t, h, near_w)

        @pl.loop(0, HEADS)
        def _(n):
            copy_to(
                kv_stage.at[n],
                kv.at[slot, quarter(part)],
                kv_send.at[n],
                kv_recv.at[slot, part],
                worker_of(n, home, core),
                here,
                start,
            )

    def send_queries(start):
        at = query_number(near_t, near_w)

        @pl.loop(0, HEADS)
        def _(n):
            copy_to(
                qg_stage.at[n],
                qg.at[at, quarter(part)],
                qg_send.at[n],
                qg_recv.at[at, part],
                worker_of(n, home, h),
                here,
                start,
            )

    send_keys(True)
    send_queries(True)

    def pass_on(kind, i, start):
        slot = KINDS[kind][0] + i
        near_t, kh, near_w = slot_at(kind, i)
        for y in range(2):
            j = 2 * y + core
            if start:
                arrived(kv.at[slot, quarter(j)], kv_recv.at[slot, j])

            def send(device, to, sem):
                copy = pltpu.make_async_remote_copy(
                    src_ref=kv.at[slot, quarter(j)],
                    dst_ref=kv.at[to, quarter(j)],
                    send_sem=sem.at[slot, y],
                    recv_sem=kv_recv.at[to, j],
                    device_id=device,
                    device_id_type=MESH,
                )
                if start:
                    copy.start()
                else:
                    copy.wait_send()

            if kind == 0:

                @pl.when(near_w == 0)
                def _():
                    send(wide_near, 12 + near_t * 2 + kh, wide_send)

            if kind in (0, 2):

                @pl.when(near_t == 0)
                def _():
                    send(time_near, 8 + near_w * 2 + kh if kind == 0 else 16 + kh, time_send)

            send(sibling, slot, relay_send)

    def relayed(slot):
        for y in range(2):
            j = 2 * y + 1 - core
            arrived(kv.at[slot, quarter(j)], kv_recv.at[slot, j])

    def score_step(kind, i):
        first, count, q0, qn = KINDS[kind]
        slot = first + i
        near_t, kh, near_w = slot_at(kind, i)
        relayed(slot)
        scores = nt(q_unit[q0 * TILE : (q0 + qn) * TILE], kv[slot, :, 0:HD])
        lows = []
        for u in range(qn):
            qt, qw = QUERY_AT[q0 + u]
            dt = absolute(T, near_t) - absolute(T, qt)
            dw = absolute(W, near_w) - absolute(W, qw)
            live = window_ref[tile_of(qt, core, qw), 9 * (dt + 1) + 3 * (kh - core + 1) + dw + 1]
            bias = (live.astype(jnp.float32) - 1.0) * 1e30
            weight = jnp.exp2(scores[u * TILE : (u + 1) * TILE] * (SCALE * LOG2E) + bias)
            rows = slice((q0 + u) * TILE, (q0 + u + 1) * TILE)
            acc[rows, HD:] += weight[:, 0:HD] + weight[:, HD : 2 * HD] + weight[:, 2 * HD :]
            lows.append(weight.astype(LOW))
        low = jnp.concatenate(lows, axis=0) if qn > 1 else lows[0]
        weights[kind][i] = low
        acc[q0 * TILE : (q0 + qn) * TILE, 0:HD] += jnp.dot(low, kv[slot, :, HD:], preferred_element_type=jnp.float32)

    def to_sibling(slot):
        return pltpu.make_async_remote_copy(
            src_ref=sib_send.at[slot],
            dst_ref=sib_recv.at[slot],
            send_sem=sib_sent.at[slot],
            recv_sem=sib_got.at[slot],
            device_id=sibling,
            device_id_type=MESH,
        )

    def send_sum(kind, i, start):
        slot = KINDS[kind][0] + i
        if kind == 0:
            owner = tile_of(*slot_at(kind, i))
            for y in range(2):
                copy_to(
                    sum_stage.at[slot, y],
                    dkv_ref.at[head],
                    sum_send.at[slot, y],
                    dkv_recv.at[head],
                    (owner, 2 * y + core),
                    here,
                    start,
                )
            return
        copy = pltpu.make_async_remote_copy(
            src_ref=sum_stage.at[slot],
            dst_ref=near_recv.at[slot - 8],
            send_sem=sum_send.at[slot, 0],
            recv_sem=near_got.at[slot - 8],
            device_id=wide_near if kind == 2 else time_near,
            device_id_type=MESH,
        )
        if start:
            copy.start()
        else:
            copy.wait_send()

    def finish_sum(kind, i):
        slot = KINDS[kind][0] + i
        near_t, kh, near_w = slot_at(kind, i)
        to_sibling(slot).wait_recv()
        for y in range(2):
            mine = quarter(2 * y + core)
            part_sum[slot % 2, mine] += sib_recv[slot, y].astype(jnp.float32)

        def add(at):
            arrived(near_recv.at[at], near_got.at[at])
            for y in range(2):
                part_sum[slot % 2, quarter(2 * y + core)] += near_recv[at, y].astype(jnp.float32)

        if kind == 0:
            pl.when(near_t == 0)(lambda: add(near_w * 2 + kh))
            pl.when(near_w == 0)(lambda: add(4 + near_t * 2 + kh))
        if kind == 2:
            pl.when(near_t == 0)(lambda: add(8 + kh))
        for y in range(2):
            sum_stage[slot, y] = part_sum[slot % 2, quarter(2 * y + core)].astype(LOW)
        send_sum(kind, i, True)

    def grad_step(kind, i):
        first, count, q0, qn = KINDS[kind]
        slot = first + i
        rows = slice(q0 * TILE, (q0 + qn) * TILE)
        low = weights[kind][i]
        prob_grad = nt(scaled[rows, 2 * HD :], kv[slot, :, HD:])
        score_grad = (low.astype(jnp.float32) * (prob_grad - thrice(row_dot[rows]))).astype(LOW)
        dq_acc[rows] += jnp.dot(score_grad, kv[slot, :, 0:HD], preferred_element_type=jnp.float32)
        part_sum[slot % 2, :, 0:HD] = tn(score_grad, scaled[rows, 0:HD])
        part_sum[slot % 2, :, HD:] = tn(low, scaled[rows, HD : 2 * HD])
        for y in range(2):
            sib_send[slot, y] = part_sum[slot % 2, quarter(2 * y + 1 - core)].astype(LOW)
        to_sibling(slot).start()

    def send_result(stage, dst, send_sem, recv_sem, start):
        for u in range(4):
            for j in range(4):
                copy_to(
                    stage.at[u, quarter(j)],
                    dst.at[:, lanes_of(head)],
                    send_sem.at[u, j],
                    recv_sem.at[head],
                    (tile_of(QUERY_AT[u][0], core, QUERY_AT[u][1]), j),
                    here,
                    start,
                )

    @pl.when(active)
    def _():
        acc[...] = jnp.zeros_like(acc)
        dq_acc[...] = jnp.zeros_like(dq_acc)

        @pl.loop(0, 8)
        def _(i):
            pass_on(0, i, True)

        for u in range(4):
            for j in range(4):
                arrived(qg.at[u, quarter(j)], qg_recv.at[u, j])
            q = qg[u, :, 0:HD].astype(jnp.float32)
            inverse = lax.rsqrt(jnp.mean(q * q, axis=-1, keepdims=True) + EPSILON)
            rows = slice(u * TILE, (u + 1) * TILE)
            q_unit[rows] = (q * inverse).astype(LOW)
            scaled[rows, 2 * HD :] = qg[u, :, HD:]

        @pl.loop(0, 8)
        def _(i):
            score_step(0, i)
            pl.when(i < 4)(lambda: pass_on(2, i, True))
            pl.when(i >= 4)(lambda: pass_on(1, i - 4, True))

        @pl.loop(0, 2)
        def _(i):
            pass_on(3, i, True)

        for kind in (2, 1, 3):

            @pl.loop(0, KINDS[kind][1])
            def _(i):
                score_step(kind, i)

        for u in range(4):
            rows = slice(u * TILE, (u + 1) * TILE)
            over[rows] = jnp.broadcast_to(1.0 / jnp.sum(acc[rows, HD:], axis=-1, keepdims=True), (TILE, HD))
            out = (acc[rows, 0:HD] * over[rows]).astype(LOW)
            o_stage[u] = out
            grad = qg[u, :, HD:].astype(jnp.float32)
            dot = jnp.sum(grad * out.astype(jnp.float32), axis=-1, keepdims=True)
            row_dot[rows] = jnp.broadcast_to(dot, (TILE, HD))
            scaled[rows, 0:HD] = (q_unit[rows].astype(jnp.float32) * (over[rows] * SCALE)).astype(LOW)
            scaled[rows, HD : 2 * HD] = (grad * over[rows]).astype(LOW)
        send_result(o_stage, o_ref, o_send, o_recv, True)

        for kind in (3, 1, 2, 0):
            count = KINDS[kind][1]

            @pl.loop(0, count)
            def _(step):
                i = count - 1 - step
                grad_step(kind, i)

                @pl.when(step > 0)
                def _():
                    finish_sum(kind, i + 1)

            finish_sum(kind, 0)

        for u in range(4):
            rows = slice(u * TILE, (u + 1) * TILE)
            q = qg[u, :, 0:HD].astype(jnp.float32)
            inverse = lax.rsqrt(jnp.mean(q * q, axis=-1, keepdims=True) + EPSILON)
            unit = q * inverse
            grad_in = dq_acc[rows] * (over[rows] * SCALE)
            dq = inverse * (grad_in - unit * jnp.mean(grad_in * unit, axis=-1, keepdims=True))
            dq_stage[u] = dq.astype(LOW)
        send_result(dq_stage, dq_ref, dq_send, dq_recv, True)

    @pl.loop(0, HEADS)
    def _(n):
        arrived(dkv_ref.at[n], dkv_recv.at[n])
        arrived(o_ref.at[:, lanes_of(n)], o_recv.at[n])
        arrived(dq_ref.at[:, lanes_of(n)], dq_recv.at[n])

    send_keys(False)
    send_queries(False)

    @pl.when(active)
    def _():
        for kind in range(4):

            @pl.loop(0, KINDS[kind][1])
            def _(i):
                pass_on(kind, i, False)
                to_sibling(KINDS[kind][0] + i).wait_send()
                send_sum(kind, i, False)

        send_result(o_stage, o_ref, o_send, o_recv, False)
        send_result(dq_stage, dq_ref, dq_send, dq_recv, False)


def finish_kernel(o_in, dq_in, dkv_in, k_in, o_ref, dq_ref, dk_ref, dv_ref, sems):
    copies = (
        pltpu.make_async_copy(o_in, o_ref, sems.at[0]),
        pltpu.make_async_copy(dq_in, dq_ref, sems.at[1]),
    )
    for copy in copies:
        copy.start()

    for n in range(HEADS):
        lanes = slice(n * HD, (n + 1) * HD)
        k = k_in[:, lanes].astype(jnp.float32)
        inverse = lax.rsqrt(jnp.mean(k * k, axis=-1, keepdims=True) + EPSILON)
        unit = k * inverse
        grad_in = dkv_in[n, :, 0:HD].astype(jnp.float32)
        dk = inverse * (grad_in - unit * jnp.mean(grad_in * unit, axis=-1, keepdims=True))
        dk_ref[:, lanes] = dk.astype(LOW)
        dv_ref[:, lanes] = dkv_in[n, :, HD:]
    for copy in copies:
        copy.wait()


def shards(queries, keys, values, out_grad, window):
    vmem = pl.BlockSpec(memory_space=pltpu.VMEM)
    smem = pl.BlockSpec(memory_space=pltpu.SMEM)
    hbm = pl.BlockSpec(memory_space=pl.ANY)
    dma = pltpu.SemaphoreType.DMA
    f32 = jnp.float32
    rows = jax.ShapeDtypeStruct((QUARTER, HEADS * HD), LOW)
    o, dq, dkv = pl.pallas_call(
        attend_kernel,
        out_shape=(rows, rows, jax.ShapeDtypeStruct((HEADS, QUARTER, 2 * HD), LOW)),
        in_specs=[smem] + [hbm] * 4,
        out_specs=(hbm,) * 3,
        scratch_shapes=[
            pltpu.VMEM((QUARTER, HEADS * HD), LOW),
            pltpu.VMEM((QUARTER, HEADS * HD), LOW),
            pltpu.VMEM((QUARTER, HEADS * HD), LOW),
            pltpu.VMEM((QUARTER, HEADS * HD), LOW),
            pltpu.VMEM((HEADS, QUARTER, 2 * HD), LOW),
            pltpu.VMEM((HEADS, QUARTER, 2 * HD), LOW),
            pltpu.VMEM((SLOTS, TILE, 2 * HD), LOW),
            pltpu.VMEM((4, TILE, 2 * HD), LOW),
            pltpu.VMEM((4 * TILE, HD), LOW),
            pltpu.VMEM((8, 4 * TILE, TILE), LOW),
            pltpu.VMEM((4, 2 * TILE, TILE), LOW),
            pltpu.VMEM((4, 2 * TILE, TILE), LOW),
            pltpu.VMEM((2, TILE, TILE), LOW),
            pltpu.VMEM((4 * TILE, 2 * HD), f32),
            pltpu.VMEM((4 * TILE, HD), f32),
            pltpu.VMEM((4 * TILE, HD), f32),
            pltpu.VMEM((4 * TILE, HD), f32),
            pltpu.VMEM((4 * TILE, 3 * HD), LOW),
            pltpu.VMEM((4, TILE, HD), LOW),
            pltpu.VMEM((4, TILE, HD), LOW),
            pltpu.VMEM((2, TILE, 2 * HD), f32),
            pltpu.VMEM((SLOTS, 2, QUARTER, 2 * HD), LOW),
            pltpu.VMEM((SLOTS, 2, QUARTER, 2 * HD), LOW),
            pltpu.VMEM((SLOTS, 2, QUARTER, 2 * HD), LOW),
            pltpu.VMEM((10, 2, QUARTER, 2 * HD), LOW),
            dma((4,)),
            dma((HEADS,)),
            dma((HEADS,)),
            dma((SLOTS, 4)),
            dma((4, 4)),
            dma((SLOTS, 2)),
            dma((SLOTS, 2)),
            dma((SLOTS, 2)),
            dma((SLOTS,)),
            dma((SLOTS,)),
            dma((10,)),
            dma((4, 4)),
            dma((4, 4)),
            dma((SLOTS, 2)),
            dma((HEADS,)),
            dma((HEADS,)),
            dma((HEADS,)),
        ],
        compiler_params=pltpu.CompilerParams(collective_id=0, has_side_effects=True, vmem_limit_bytes=VMEM_LIMIT),
        name="attend",
    )(window, queries, keys, values, out_grad)

    return pl.pallas_call(
        finish_kernel,
        out_shape=(rows,) * 4,
        in_specs=[hbm, hbm, vmem, vmem],
        out_specs=(hbm, hbm, vmem, vmem),
        scratch_shapes=[dma((2,))],
        compiler_params=pltpu.CompilerParams(vmem_limit_bytes=8 * 1024 * 1024),
        name="finish",
    )(o, dq, dkv, keys)


def solution(mesh):
    rows = P(("tm", "head"), None)
    return jax.shard_map(
        shards, mesh=mesh, in_specs=(rows, rows, rows, rows, P()), out_specs=(rows, rows, rows, rows), check_vma=False
    )
```

time: 118 us -> 92 us (0.78)
  Pallas kernels: 113 us -> 88.1 us
  local copies, waits for them, and re-layouts: 4.59 us -> 2.98 us
    pallas_call x1 -> x2, Pallas kernels: 113 us -> 88.1 us  [the longest x1 86.5 us: shards(): pl.pallas_call(attend_kernel, out_shape=(rows, rows, jax.ShapeDtypeStruct...]
    unnamed x10 -> x8, local copies, waits for them, and re-layouts: 4.59 us -> 2.98 us
where the time goes in v3:
time: 92 us; the launch traced here: 91.7 us
  Pallas kernels  88.1 us (96%)
  local copies, waits for them, and re-layouts  2.98 us (3%)
    pallas_call x1, Pallas kernels, shards(): pl.pallas_call(attend_kernel, out_shape=(rows, rows, jax.ShapeDtypeStruct...  86.5 us
    unnamed x8, local copies, waits for them, and re-layouts  2.98 us

profile of v3, /device:TPU:29, one launch (start us, length us, event | category | flops | bytes accessed | tf_op | source)
XLA Modules:
  0.0 91.7 jit_solution(18334632355154412456)
XLA Ops:
  0.6 0.0 copy-start
  0.6 86.5 %attend.1 = (bf16[96,1536]{1,0:T(8,128)(2,1)}, bf16[96,1536]{1,0:T(8,128)(2,1)}, bf16[12,96,256]{2,1,0:T(8,128)(2,1)}) custom-call(s32[32,27]{1,0:T(8,128)} %window_ref.1, bf16[96,1536]{1,0:T(8,128)(2,1)} %q_hbm.1, bf16[96,1536]{1,0:T(8,128)(2,1)} %k_in.1, bf16[96,1536]{1,0:T(8,128)(2,1)} %v_hbm.1, bf16[96,1536]{1,0:T(8,128)(2,1)} %g_hbm.1), custom_call_target="tpu_custom_call" | custom-call | tf_op jit(solution)/shard_map/attend/pallas_call | solution.py:562
  87.1 0.0 copy-done
  87.1 0.0 copy-start.1
  87.1 1.1 %copy-done.1 = bf16[12,96,256]{2,1,0:T(8,128)(2,1)S(1)} copy-done((bf16[12,96,256]{2,1,0:T(8,128)(2,1)S(1)}, bf16[12,96,256]{2,1,0:T(8,128)(2,1)}, u32[]{:S(2)}) %copy-start.1) | copy-done | bytes 589848
  88.2 0.0 copy-start.2
  88.2 1.0 %copy-done.2 = bf16[96,1536]{1,0:T(8,128)(2,1)S(1)} copy-done((bf16[96,1536]{1,0:T(8,128)(2,1)S(1)}, bf16[96,1536]{1,0:T(8,128)(2,1)}, u32[]{:S(2)}) %copy-start.2) | copy-done | bytes 294936
  89.1 0.0 copy-start.3
  89.1 1.0 %copy-done.3 = bf16[96,1536]{1,0:T(8,128)(2,1)S(1)} copy-done((bf16[96,1536]{1,0:T(8,128)(2,1)S(1)}, bf16[96,1536]{1,0:T(8,128)(2,1)}, u32[]{:S(2)}) %copy-start.3) | copy-done | bytes 294936
  90.1 1.6 %finish.1 = (bf16[96,1536]{1,0:T(8,128)(2,1)}, bf16[96,1536]{1,0:T(8,128)(2,1)}, bf16[96,1536]{1,0:T(8,128)(2,1)}, bf16[96,1536]{1,0:T(8,128)(2,1)}) custom-call(bf16[96,1536]{1,0:T(8,128)(2,1)S(1)} %copy-done.2, bf16[96,1536]{1,0:T(8,128)(2,1)S(1)} %copy-done.3, bf16[12,96,256]{2,1,0:T(8,128)(2,1)S(1)} %copy-done.1, bf16[96,1536]{1,0:T(8,128)(2,1)S(1)} %copy-done), custom_call_target="tpu_custom_call" | custom-call | tf_op jit(solution)/shard_map/finish/pallas_call | solution.py:615
Async XLA Ops:
  0.6 86.5 %copy-start = (bf16[96,1536]{1,0:T(8,128)(2,1)S(1)}, bf16[96,1536]{1,0:T(8,128)(2,1)}, u32[]{:S(2)}) copy-start(bf16[96,1536]{1,0:T(8,128)(2,1)} %k_in.1) | copy-start | bytes 884740
  87.1 1.1 %copy-start.1 = (bf16[12,96,256]{2,1,0:T(8,128)(2,1)S(1)}, bf16[12,96,256]{2,1,0:T(8,128)(2,1)}, u32[]{:S(2)}) copy-start(bf16[12,96,256]{2,1,0:T(8,128)(2,1)} %get-tuple-element.9.dkv_in) | copy-start | bytes 1769476
  88.2 1.0 %copy-start.2 = (bf16[96,1536]{1,0:T(8,128)(2,1)S(1)}, bf16[96,1536]{1,0:T(8,128)(2,1)}, u32[]{:S(2)}) copy-start(bf16[96,1536]{1,0:T(8,128)(2,1)} %get-tuple-element.7.o_in) | copy-start | bytes 884740
  89.1 1.0 %copy-start.3 = (bf16[96,1536]{1,0:T(8,128)(2,1)S(1)}, bf16[96,1536]{1,0:T(8,128)(2,1)}, u32[]{:S(2)}) copy-start(bf16[96,1536]{1,0:T(8,128)(2,1)} %get-tuple-element.8.dq_in) | copy-start | bytes 884740

commit v4 on v3

v4 whole, which is shorter than its diff:
```python
import jax
import jax.numpy as jnp
from jax import lax
from jax.experimental import pallas as pl
from jax.experimental.pallas import tpu as pltpu
from jax.sharding import PartitionSpec as P

TILE = 384
HEADS = 12
HD = 128
QUARTER = 96
SLOTS = 18
LAG = 3
EPSILON = 1e-06
SCALE = HD**-0.5
LOG2E = 1.4426950408889634
MESH = pl.DeviceIdType.MESH
VMEM_LIMIT = 60 * 1024 * 1024
LOW = jnp.bfloat16

QUERY_AT = ((0, 1), (0, 0), (1, 0), (1, 1))
KINDS = ((0, 8, 0, 4), (8, 4, 0, 2), (12, 4, 1, 2), (16, 2, 1, 1))

def worker_of(n, T, W, core):
    y = n % 4
    spot = (n // 4 + y + 1) % 4
    x, z = absolute(T, spot // 2), 2 * (spot % 2) + W
    return x * 8 + z * 2 + y // 2, (y % 2) * 2 + core


def work_here(tm, part):
    x, y, z = tm // 8, tm % 2 * 2 + part // 2, tm // 2 % 4
    T, W = x // 2, z % 2
    row = (relative(T, x) * 2 + z // 2 + 7 - y) % 4
    return row < 3, jnp.where(row < 3, row * 4 + y, 0), T, W, part % 2


def absolute(half, near):
    return 1 + half + near * (2 * half - 1)


def relative(half, index):
    return (index - 1 - half) * (2 * half - 1)


def slot_at(kind, i):
    if kind == 0:
        return i // 4, i % 2, i // 2 % 2
    if kind == 1:
        return -1, i % 2, i // 2
    if kind == 2:
        return i // 2, i % 2, -1
    return -1, i % 2, -1


def slot_number(near_t, h, near_w):
    return jnp.where(
        near_t >= 0,
        jnp.where(near_w >= 0, (near_t * 2 + near_w) * 2 + h, 12 + near_t * 2 + h),
        jnp.where(near_w >= 0, 8 + near_w * 2 + h, 16 + h),
    )


def query_number(near_t, near_w):
    return jnp.where(near_t == 0, 1 - near_w, 2 + near_w)


def copy_to(src, dst, send_sem, recv_sem, device, here):
    same = (device[0] == here[0]) & (device[1] == here[1])

    @pl.when(same)
    def _():
        pltpu.make_async_copy(src, dst, recv_sem).start()

    @pl.when(jnp.logical_not(same))
    def _():
        pltpu.make_async_remote_copy(
            src_ref=src, dst_ref=dst, send_sem=send_sem, recv_sem=recv_sem, device_id=device, device_id_type=MESH
        ).start()


def arrived(ref, sem):
    pltpu.make_async_copy(ref, ref, sem).wait()


def nt(a, b):
    return lax.dot_general(a, b, (((1,), (1,)), ((), ())), preferred_element_type=jnp.float32)


def tn(a, b):
    return lax.dot_general(a, b, (((0,), (0,)), ((), ())), preferred_element_type=jnp.float32)


def quarter(j):
    return pl.ds(pl.multiple_of(j * QUARTER, QUARTER), QUARTER)


def lanes_of(n):
    return pl.ds(pl.multiple_of(n * HD, HD), HD)


def thrice(value):
    return jnp.concatenate([value] * 3, axis=1)


def attend_kernel(
    window_ref,
    q_hbm,
    k_hbm,
    v_hbm,
    g_hbm,
    o_ref,
    dq_ref,
    dkv_ref,
    q_in,
    k_in,
    v_in,
    g_in,
    kv_stage,
    qg_stage,
    kv,
    qg,
    q_unit,
    weights0,
    weights1,
    weights2,
    weights3,
    acc,
    dq_acc,
    over,
    row_dot,
    scaled,
    o_stage,
    dq_stage,
    part_sum,
    sib_send,
    sib_recv,
    sum_stage,
    near_recv,
    in_sem,
    kv_send,
    qg_send,
    kv_recv,
    qg_recv,
    relay_send,
    time_send,
    wide_send,
    sib_sent,
    sib_got,
    near_got,
    o_send,
    dq_send,
    sum_send,
    o_recv,
    dq_recv,
    dkv_recv,
):
    tm, part = lax.axis_index("tm"), lax.axis_index("head")
    here = (tm, part)
    t, h, w = tm // 8, tm // 4 % 2, tm % 4
    active, head, T, W, core = work_here(tm, part)
    home_t, home_w = t // 2, w // 2
    own_t, own_w = relative(home_t, t), relative(home_w, w)
    sibling = (tm, part + 1 - 2 * core)
    time_near = worker_of(head, 1 - T, W, core)
    wide_near = worker_of(head, T, 1 - W, core)
    weights = (weights0, weights1, weights2, weights3)

    def copy_in(i):
        return pltpu.make_async_copy((k_hbm, v_hbm, q_hbm, g_hbm)[i], (k_in, v_in, q_in, g_in)[i], in_sem.at[i])

    for i in range(4):
        copy_in(i).start()

    def tile_of(near_t, kh, near_w):
        return absolute(T, near_t) * 8 + kh * 4 + absolute(W, near_w)

    barrier = pltpu.get_barrier_semaphore()

    def greet(device, count):
        other = jnp.logical_not((device[0] == tm) & (device[1] == part))

        @pl.when(other)
        def _():
            pl.semaphore_signal(barrier, inc=1, device_id=device, device_id_type=MESH)

        return count + other.astype(jnp.int32)

    def greet_workers(n, count):
        count = greet(worker_of(n, home_t, home_w, core), count)
        return lax.cond(h != core, lambda c: greet(worker_of(n, home_t, home_w, h), c), lambda c: c, count)

    greeted = lax.fori_loop(0, HEADS, greet_workers, jnp.int32(0))

    def greet_owners(i, count):
        near_t, kh, near_w = slot_at(0, i)
        owner = tile_of(near_t, kh, near_w)
        for y in range(2):
            count = greet((owner, 2 * y + core), count)

        def others(count):
            for y in range(2):
                count = greet((owner, 2 * y + 1 - core), count)
            return count

        return lax.cond(kh == core, others, lambda count: count, count)

    def greet_all(count):
        count = lax.fori_loop(0, 8, greet_owners, count)
        for device in (sibling, time_near, wide_near):
            count = greet(device, count)
        return count

    greeted = lax.cond(active, greet_all, lambda count: count, greeted)

    copy_in(0).wait()
    copy_in(1).wait()

    @pl.loop(0, HEADS)
    def _(n):
        lanes = lanes_of(n)
        k = k_in[:, lanes].astype(jnp.float32)
        inverse = lax.rsqrt(jnp.mean(k * k, axis=-1, keepdims=True) + EPSILON)
        kv_stage[n, :, 0:HD] = (k * inverse).astype(LOW)
        kv_stage[n, :, HD:] = v_in[:, lanes]

    copy_in(2).wait()
    copy_in(3).wait()

    @pl.loop(0, HEADS)
    def _(n):
        lanes = lanes_of(n)
        qg_stage[n, :, 0:HD] = q_in[:, lanes]
        qg_stage[n, :, HD:] = g_in[:, lanes]

    pl.semaphore_wait(barrier, greeted)

    def send_keys():
        slot = (own_t * 2 + own_w) * 2 + h

        @pl.loop(0, HEADS)
        def _(n):
            copy_to(
                kv_stage.at[n],
                kv.at[slot, quarter(part)],
                kv_send,
                kv_recv.at[slot, part],
                worker_of(n, home_t, home_w, core),
                here,
            )

    def send_queries():
        at = query_number(own_t, own_w)

        @pl.loop(0, HEADS)
        def _(n):
            copy_to(
                qg_stage.at[n],
                qg.at[at, quarter(part)],
                qg_send,
                qg_recv,
                worker_of(n, home_t, home_w, h),
                here,
            )

    pl.when(own_t == 0)(send_keys)
    send_queries()
    pl.when(own_t != 0)(send_keys)

    def pass_on(kind, i):
        slot = KINDS[kind][0] + i
        near_t, kh, near_w = slot_at(kind, i)
        for y in range(2):
            j = 2 * y + core
            arrived(kv.at[slot, quarter(j)], kv_recv.at[slot, j])

            def send(device, to, sem):
                pltpu.make_async_remote_copy(
                    src_ref=kv.at[slot, quarter(j)],
                    dst_ref=kv.at[to, quarter(j)],
                    send_sem=sem,
                    recv_sem=kv_recv.at[to, j],
                    device_id=device,
                    device_id_type=MESH,
                ).start()

            if kind == 0:

                @pl.when(near_w == 0)
                def _():
                    send(wide_near, 12 + near_t * 2 + kh, wide_send)

            if kind in (0, 2):

                @pl.when(near_t == 0)
                def _():
                    send(time_near, 8 + near_w * 2 + kh if kind == 0 else 16 + kh, time_send)

            send(sibling, slot, relay_send)

    def relayed(slot):
        for y in range(2):
            j = 2 * y + 1 - core
            arrived(kv.at[slot, quarter(j)], kv_recv.at[slot, j])

    def score_step(kind, i):
        first, count, q0, qn = KINDS[kind]
        slot = first + i
        near_t, kh, near_w = slot_at(kind, i)
        relayed(slot)
        scores = nt(q_unit[q0 * TILE : (q0 + qn) * TILE], kv[slot, :, 0:HD])
        lows = []
        for u in range(qn):
            qt, qw = QUERY_AT[q0 + u]
            dt = absolute(T, near_t) - absolute(T, qt)
            dw = absolute(W, near_w) - absolute(W, qw)
            live = window_ref[tile_of(qt, core, qw), 9 * (dt + 1) + 3 * (kh - core + 1) + dw + 1]
            bias = (live.astype(jnp.float32) - 1.0) * 1e30
            weight = jnp.exp2(scores[u * TILE : (u + 1) * TILE] * (SCALE * LOG2E) + bias)
            rows = slice((q0 + u) * TILE, (q0 + u + 1) * TILE)
            acc[rows, HD:] += weight[:, 0:HD] + weight[:, HD : 2 * HD] + weight[:, 2 * HD :]
            lows.append(weight.astype(LOW))
        low = jnp.concatenate(lows, axis=0) if qn > 1 else lows[0]
        weights[kind][i] = low
        acc[q0 * TILE : (q0 + qn) * TILE, 0:HD] += jnp.dot(low, kv[slot, :, HD:], preferred_element_type=jnp.float32)

    def to_sibling(slot):
        return pltpu.make_async_remote_copy(
            src_ref=sib_send.at[slot],
            dst_ref=sib_recv.at[slot],
            send_sem=sib_sent,
            recv_sem=sib_got.at[slot],
            device_id=sibling,
            device_id_type=MESH,
        )

    def send_sum(slot):
        @pl.when(slot < 8)
        def _():
            owner = tile_of(*slot_at(0, slot))
            for y in range(2):
                copy_to(
                    sum_stage.at[slot, y],
                    dkv_ref.at[head],
                    sum_send,
                    dkv_recv,
                    (owner, 2 * y + core),
                    here,
                )

        def pass_back(device):
            pltpu.make_async_remote_copy(
                src_ref=sum_stage.at[slot],
                dst_ref=near_recv.at[slot - 8],
                send_sem=sum_send,
                recv_sem=near_got.at[slot - 8],
                device_id=device,
                device_id_type=MESH,
            ).start()

        wide = (slot >= 12) & (slot < 16)
        pl.when(wide)(lambda: pass_back(wide_near))
        pl.when((slot >= 8) & jnp.logical_not(wide))(lambda: pass_back(time_near))

    def taken(g):
        own = (17 - g) % 8
        return jnp.where(g < 2, 17 - g, jnp.where(g < 6, 13 - g, jnp.where(g < 10, 21 - g, own)))

    def wait_terms(slot):
        to_sibling(slot).wait_recv()
        for at in near_terms(slot):
            pl.when(at < 10)(lambda at=at: arrived(near_recv.at[at], near_got.at[at]))

    def near_terms(slot):
        near_t, kh, near_w = slot_at(0, slot)
        own = slot < 8
        time_at = jnp.where(own & (near_t == 0), near_w * 2 + kh, 10)
        wide_at = jnp.where(own & (near_w == 0), 4 + near_t * 2 + kh, 10)
        return time_at, jnp.where((slot == 12) | (slot == 13), slot - 4, wide_at)

    def add_terms(slot, held):
        terms = near_terms(slot)
        for y in range(2):
            total = part_sum[held, quarter(2 * y + core)] + sib_recv[slot, y].astype(jnp.float32)
            for at in terms:
                total += near_recv[at, y].astype(jnp.float32)
            sum_stage[slot, y] = total.astype(LOW)

    def finish_sum(g):
        slot = taken(g)
        wait_terms(slot)
        add_terms(slot, g % (LAG + 1))
        send_sum(slot)

    def grad_step(kind, g):
        first, count, q0, qn = KINDS[kind]
        slot = taken(g)
        i = slot - first
        held = g % (LAG + 1)
        done = g >= LAG
        before = jnp.where(done, taken(g - LAG), SLOTS)
        rows = slice(q0 * TILE, (q0 + qn) * TILE)
        pl.when(done)(lambda: wait_terms(before))
        add_terms(before, (g + 1) % (LAG + 1))
        low = weights[kind][i]
        prob_grad = nt(scaled[rows, 2 * HD :], kv[slot, :, HD:])
        score_grad = (low.astype(jnp.float32) * (prob_grad - thrice(row_dot[rows]))).astype(LOW)
        dq_acc[rows] += jnp.dot(score_grad, kv[slot, :, 0:HD], preferred_element_type=jnp.float32)
        part_sum[held, :, 0:HD] = tn(score_grad, scaled[rows, 0:HD])
        part_sum[held, :, HD:] = tn(low, scaled[rows, HD : 2 * HD])
        for y in range(2):
            sib_send[slot, y] = part_sum[held, quarter(2 * y + 1 - core)].astype(LOW)
        to_sibling(slot).start()
        pl.when(done)(lambda: send_sum(before))

    def send_result(stage, dst, send_sem, recv_sem):
        for u in range(4):
            for j in range(4):
                copy_to(
                    stage.at[u, quarter(j)],
                    dst.at[:, lanes_of(head)],
                    send_sem,
                    recv_sem,
                    (tile_of(QUERY_AT[u][0], core, QUERY_AT[u][1]), j),
                    here,
                )

    @pl.when(active)
    def _():
        acc[...] = jnp.zeros_like(acc)
        dq_acc[...] = jnp.zeros_like(dq_acc)
        near_recv[10] = jnp.zeros((2, QUARTER, 2 * HD), LOW)
        sib_recv[SLOTS] = jnp.zeros((2, QUARTER, 2 * HD), LOW)

        @pl.loop(0, 4)
        def _(i):
            pass_on(0, i)

        @pl.loop(0, 2)
        def _(i):
            pass_on(2, i)

        arrived(qg, qg_recv)
        for u in range(4):
            q = qg[u, :, 0:HD].astype(jnp.float32)
            inverse = lax.rsqrt(jnp.mean(q * q, axis=-1, keepdims=True) + EPSILON)
            rows = slice(u * TILE, (u + 1) * TILE)
            q_unit[rows] = (q * inverse).astype(LOW)
            scaled[rows, 2 * HD :] = qg[u, :, HD:]

        @pl.loop(0, 8)
        def _(i):
            score_step(0, i)
            pl.when(i < 4)(lambda: pass_on(0, i + 4))
            pl.when(i >= 4)(lambda: pass_on(1, i - 4))
            pl.when(i >= 6)(lambda: pass_on(2, i - 4))

        @pl.loop(0, 2)
        def _(i):
            pass_on(3, i)

        for kind in (2, 1, 3):

            @pl.loop(0, KINDS[kind][1])
            def _(i):
                score_step(kind, i)

        for u in range(4):
            rows = slice(u * TILE, (u + 1) * TILE)
            over[rows] = jnp.broadcast_to(1.0 / jnp.sum(acc[rows, HD:], axis=-1, keepdims=True), (TILE, HD))
            out = (acc[rows, 0:HD] * over[rows]).astype(LOW)
            o_stage[u] = out
            grad = qg[u, :, HD:].astype(jnp.float32)
            dot = jnp.sum(grad * out.astype(jnp.float32), axis=-1, keepdims=True)
            row_dot[rows] = jnp.broadcast_to(dot, (TILE, HD))
            scaled[rows, 0:HD] = (q_unit[rows].astype(jnp.float32) * (over[rows] * SCALE)).astype(LOW)
            scaled[rows, HD : 2 * HD] = (grad * over[rows]).astype(LOW)
        send_result(o_stage, o_ref, o_send, o_recv)

        for kind, start in ((3, 0), (1, 2), (2, 6), (0, 10)):

            @pl.loop(start, start + KINDS[kind][1])
            def _(g):
                grad_step(kind, g)

        finish_sum(SLOTS - 3)
        for u in range(4):
            rows = slice(u * TILE, (u + 1) * TILE)
            q = qg[u, :, 0:HD].astype(jnp.float32)
            inverse = lax.rsqrt(jnp.mean(q * q, axis=-1, keepdims=True) + EPSILON)
            unit = q * inverse
            grad_in = dq_acc[rows] * (over[rows] * SCALE)
            dq = inverse * (grad_in - unit * jnp.mean(grad_in * unit, axis=-1, keepdims=True))
            dq_stage[u] = dq.astype(LOW)
        finish_sum(SLOTS - 2)
        finish_sum(SLOTS - 1)
        send_result(dq_stage, dq_ref, dq_send, dq_recv)

    arrived(dkv_ref, dkv_recv)
    arrived(o_ref, o_recv)
    arrived(dq_ref, dq_recv)

    def left(ref, sem, kept, own):
        pl.when(kept)(lambda: arrived(ref.at[pl.ds(0, own)], sem))
        pl.when(jnp.logical_not(kept))(lambda: arrived(ref, sem))

    left(kv_stage, kv_send, active, HEADS - 1)
    left(qg_stage, qg_send, active & (h == core), HEADS - 1)

    @pl.when(active)
    def _():
        arrived(sib_send, relay_send)
        arrived(sib_send.at[pl.ds(0, 6)], time_send)
        arrived(sib_send.at[pl.ds(0, 4)], wide_send)
        arrived(sib_send, sib_sent)
        arrived(sib_send.at[pl.ds(0, SLOTS - 1)], sum_send)
        arrived(sib_send.at[0, 0], sum_send)
        for stage, sem in ((o_stage, o_send), (dq_stage, dq_send)):
            arrived(stage.at[pl.ds(0, 3)], sem)
            arrived(stage.at[3, pl.ds(0, 3 * QUARTER)], sem)
            pl.when(h != core)(lambda: arrived(stage.at[3, quarter(3)], sem))


def finish_kernel(o_in, dq_in, dkv_in, k_in, o_ref, dq_ref, dk_ref, dv_ref):
    o_ref[...] = o_in[...]
    dq_ref[...] = dq_in[...]
    for n in range(HEADS):
        lanes = slice(n * HD, (n + 1) * HD)
        k = k_in[:, lanes].astype(jnp.float32)
        inverse = lax.rsqrt(jnp.mean(k * k, axis=-1, keepdims=True) + EPSILON)
        unit = k * inverse
        grad_in = dkv_in[n, :, 0:HD].astype(jnp.float32)
        dk = inverse * (grad_in - unit * jnp.mean(grad_in * unit, axis=-1, keepdims=True))
        dk_ref[:, lanes] = dk.astype(LOW)
        dv_ref[:, lanes] = dkv_in[n, :, HD:]


def shards(queries, keys, values, out_grad, window):
    vmem = pl.BlockSpec(memory_space=pltpu.VMEM)
    smem = pl.BlockSpec(memory_space=pltpu.SMEM)
    hbm = pl.BlockSpec(memory_space=pl.ANY)
    dma = pltpu.SemaphoreType.DMA
    f32 = jnp.float32
    rows = jax.ShapeDtypeStruct((QUARTER, HEADS * HD), LOW)
    o, dq, dkv = pl.pallas_call(
        attend_kernel,
        out_shape=(rows, rows, jax.ShapeDtypeStruct((HEADS, QUARTER, 2 * HD), LOW)),
        in_specs=[smem] + [hbm] * 4,
        out_specs=(hbm,) * 3,
        scratch_shapes=[
            pltpu.VMEM((QUARTER, HEADS * HD), LOW),
            pltpu.VMEM((QUARTER, HEADS * HD), LOW),
            pltpu.VMEM((QUARTER, HEADS * HD), LOW),
            pltpu.VMEM((QUARTER, HEADS * HD), LOW),
            pltpu.VMEM((HEADS, QUARTER, 2 * HD), LOW),
            pltpu.VMEM((HEADS, QUARTER, 2 * HD), LOW),
            pltpu.VMEM((SLOTS, TILE, 2 * HD), LOW),
            pltpu.VMEM((4, TILE, 2 * HD), LOW),
            pltpu.VMEM((4 * TILE, HD), LOW),
            pltpu.VMEM((8, 4 * TILE, TILE), LOW),
            pltpu.VMEM((4, 2 * TILE, TILE), LOW),
            pltpu.VMEM((4, 2 * TILE, TILE), LOW),
            pltpu.VMEM((2, TILE, TILE), LOW),
            pltpu.VMEM((4 * TILE, 2 * HD), f32),
            pltpu.VMEM((4 * TILE, HD), f32),
            pltpu.VMEM((4 * TILE, HD), f32),
            pltpu.VMEM((4 * TILE, HD), f32),
            pltpu.VMEM((4 * TILE, 3 * HD), LOW),
            pltpu.VMEM((4, TILE, HD), LOW),
            pltpu.VMEM((4, TILE, HD), LOW),
            pltpu.VMEM((LAG + 1, TILE, 2 * HD), f32),
            pltpu.VMEM((SLOTS, 2, QUARTER, 2 * HD), LOW),
            pltpu.VMEM((SLOTS + 1, 2, QUARTER, 2 * HD), LOW),
            pltpu.VMEM((SLOTS + 1, 2, QUARTER, 2 * HD), LOW),
            pltpu.VMEM((11, 2, QUARTER, 2 * HD), LOW),
            dma((4,)),
            pltpu.SemaphoreType.DMA,
            pltpu.SemaphoreType.DMA,
            dma((SLOTS, 4)),
            pltpu.SemaphoreType.DMA,
            pltpu.SemaphoreType.DMA,
            pltpu.SemaphoreType.DMA,
            pltpu.SemaphoreType.DMA,
            pltpu.SemaphoreType.DMA,
            dma((SLOTS,)),
            dma((10,)),
            pltpu.SemaphoreType.DMA,
            pltpu.SemaphoreType.DMA,
            pltpu.SemaphoreType.DMA,
            pltpu.SemaphoreType.DMA,
            pltpu.SemaphoreType.DMA,
            pltpu.SemaphoreType.DMA,
        ],
        compiler_params=pltpu.CompilerParams(collective_id=0, has_side_effects=True, vmem_limit_bytes=VMEM_LIMIT),
        name="attend",
    )(window, queries, keys, values, out_grad)

    return pl.pallas_call(
        finish_kernel,
        out_shape=(rows,) * 4,
        in_specs=[vmem] * 4,
        out_specs=(vmem,) * 4,
        compiler_params=pltpu.CompilerParams(vmem_limit_bytes=VMEM_LIMIT),
        name="finish",
    )(o, dq, dkv, keys)


def solution(mesh):
    rows = P(("tm", "head"), None)
    return jax.shard_map(
        shards, mesh=mesh, in_specs=(rows, rows, rows, rows, P()), out_specs=(rows, rows, rows, rows), check_vma=False
    )
```

time: 92 us -> 87.1 us (0.947); the launches traced: 91.7 us -> 85.9 us
  local copies, waits for them, and re-layouts: 2.98 us -> 0 us
  Pallas kernels: 88.1 us -> 85.2 us
    pallas_call x1, Pallas kernels: 86.5 us -> 82.2 us  [shards(): pl.pallas_call(attend_kernel, out_shape=(rows, rows, jax.ShapeDtypeStruct...]
    unnamed x8 -> x0, local copies, waits for them, and re-layouts: 2.98 us -> none
    pallas_call x1, Pallas kernels: 1.64 us -> 3.01 us  [shards(): pl.pallas_call(finish_kernel, out_shape=(rows,) * 4, in_specs=[vmem] * 4,...]
where the time goes in v4:
time: 87.1 us; the launch traced here: 85.9 us
  Pallas kernels  85.2 us (98%)
    pallas_call x1, Pallas kernels, shards(): pl.pallas_call(attend_kernel, out_shape=(rows, rows, jax.ShapeDtypeStruct...  82.2 us
    pallas_call x1, Pallas kernels, shards(): pl.pallas_call(finish_kernel, out_shape=(rows,) * 4, in_specs=[vmem] * 4,...  3.01 us

profile of v4, /device:TPU:29, one launch (start us, length us, event | category | flops | bytes accessed | tf_op | source)
XLA Modules:
  0.0 85.9 jit_solution(15100478087208198635)
XLA Ops:
  0.6 82.2 %attend.1 = (bf16[96,1536]{1,0:T(8,128)(2,1)}, bf16[96,1536]{1,0:T(8,128)(2,1)}, bf16[12,96,256]{2,1,0:T(8,128)(2,1)}) custom-call(s32[32,27]{1,0:T(8,128)} %window_ref.1, bf16[96,1536]{1,0:T(8,128)(2,1)} %q_hbm.1, bf16[96,1536]{1,0:T(8,128)(2,1)} %k_in.1, bf16[96,1536]{1,0:T(8,128)(2,1)} %v_hbm.1, bf16[96,1536]{1,0:T(8,128)(2,1)} %g_hbm.1), custom_call_target="tpu_custom_call" | custom-call | tf_op jit(solution)/shard_map/attend/pallas_call | solution.py:545
  82.8 3.0 %finish.1 = (bf16[96,1536]{1,0:T(8,128)(2,1)}, bf16[96,1536]{1,0:T(8,128)(2,1)}, bf16[96,1536]{1,0:T(8,128)(2,1)}, bf16[96,1536]{1,0:T(8,128)(2,1)}) custom-call(bf16[96,1536]{1,0:T(8,128)(2,1)} %get-tuple-element.7.o_in, bf16[96,1536]{1,0:T(8,128)(2,1)} %get-tuple-element.8.dq_in, bf16[12,96,256]{2,1,0:T(8,128)(2,1)} %get-tuple-element.9.dkv_in, ...), custom_call_target="tpu_custom_call" | custom-call | tf_op jit(solution)/shard_map/finish/pallas_call | solution.py:598

commit v5 on v4

v5 whole, which is shorter than its diff:
```python
import jax
import jax.numpy as jnp
from jax import lax
from jax.experimental import pallas as pl
from jax.experimental.pallas import tpu as pltpu
from jax.sharding import PartitionSpec as P

TILE = 384
HEADS = 12
HD = 128
QUARTER = 96
PAIR = 768
SLOTS = 9
LAG = 1
EPSILON = 1e-06
SCALE = HD**-0.5
LOG2E = 1.4426950408889634
MESH = pl.DeviceIdType.MESH
VMEM_LIMIT = 60 * 1024 * 1024
LOW = jnp.bfloat16

QUERY_AT = ((0, 1), (0, 0), (1, 0), (1, 1))
KINDS = ((0, 4, 0, 4), (4, 2, 0, 2), (6, 2, 1, 2), (8, 1, 1, 1))


def worker_of(n, T, W, core):
    y = n % 4
    spot = (n // 4 + y + 1) % 4
    x, z = absolute(T, spot // 2), 2 * (spot % 2) + W
    return x * 8 + z * 2 + y // 2, (y % 2) * 2 + core


def work_here(tm, part):
    x, y, z = tm // 8, tm % 2 * 2 + part // 2, tm // 2 % 4
    T, W = x // 2, z % 2
    row = (relative(T, x) * 2 + z // 2 + 7 - y) % 4
    return row < 3, jnp.where(row < 3, row * 4 + y, 0), T, W, part % 2


def absolute(half, near):
    return 1 + half + near * (2 * half - 1)


def relative(half, index):
    return (index - 1 - half) * (2 * half - 1)


def pair_at(kind, i):
    if kind == 0:
        return i // 2, i % 2
    if kind == 1:
        return -1, i
    if kind == 2:
        return i, -1
    return -1, -1


def query_number(near_t, near_w):
    return jnp.where(near_t == 0, 1 - near_w, 2 + near_w)


def copy_to(src, dst, send_sem, recv_sem, device, here):
    same = (device[0] == here[0]) & (device[1] == here[1])

    @pl.when(same)
    def _():
        pltpu.make_async_copy(src, dst, recv_sem).start()

    @pl.when(jnp.logical_not(same))
    def _():
        pltpu.make_async_remote_copy(
            src_ref=src, dst_ref=dst, send_sem=send_sem, recv_sem=recv_sem, device_id=device, device_id_type=MESH
        ).start()


def arrived(ref, sem):
    pltpu.make_async_copy(ref, ref, sem).wait()


def nt(a, b):
    return lax.dot_general(a, b, (((1,), (1,)), ((), ())), preferred_element_type=jnp.float32)


def quarter(j):
    return pl.ds(pl.multiple_of(j * QUARTER, QUARTER), QUARTER)


def half(core):
    return pl.ds(pl.multiple_of(core * TILE, TILE), TILE)


def lanes_of(n):
    return pl.ds(pl.multiple_of(n * HD, HD), HD)


def repeated(value):
    return jnp.concatenate([value] * (PAIR // HD), axis=1)


def attend_kernel(
    window_hbm,
    q_hbm,
    k_hbm,
    v_hbm,
    g_hbm,
    o_ref,
    dq_ref,
    dkv_ref,
    window_ref,
    q_in,
    k_in,
    v_in,
    g_in,
    kv_stage,
    qg_stage,
    kv,
    qg,
    q_unit,
    weights0,
    weights1,
    weights2,
    weights3,
    acc,
    dq_acc,
    over,
    row_dot,
    scaled,
    grad_rows,
    o_stage,
    dq_stage,
    part_sum,
    sib_send,
    sib_recv,
    sum_stage,
    near_recv,
    in_sem,
    kv_send,
    qg_send,
    kv_recv,
    qg_recv,
    relay_send,
    time_send,
    wide_send,
    sib_sent,
    sib_got,
    near_got,
    o_send,
    dq_send,
    sum_send,
    o_recv,
    dq_recv,
    dkv_recv,
):
    tm, part = lax.axis_index("tm"), lax.axis_index("head")
    here = (tm, part)
    t, h, w = tm // 8, tm // 4 % 2, tm % 4
    active, head, T, W, core = work_here(tm, part)
    home_t, home_w = t // 2, w // 2
    own_t, own_w = relative(home_t, t), relative(home_w, w)
    sibling = (tm, part + 1 - 2 * core)
    time_near = worker_of(head, 1 - T, W, core)
    wide_near = worker_of(head, T, 1 - W, core)
    weights = (weights0, weights1, weights2, weights3)

    def copy_in(i):
        source = (k_hbm, v_hbm, q_hbm, g_hbm, window_hbm)[i]
        return pltpu.make_async_copy(source, (k_in, v_in, q_in, g_in, window_ref)[i], in_sem.at[i])

    for i in range(5):
        copy_in(i).start()

    def tile_of(near_t, kh, near_w):
        return absolute(T, near_t) * 8 + kh * 4 + absolute(W, near_w)

    barrier = pltpu.get_barrier_semaphore()

    def greet(device, count):
        other = jnp.logical_not((device[0] == tm) & (device[1] == part))

        @pl.when(other)
        def _():
            pl.semaphore_signal(barrier, inc=1, device_id=device, device_id_type=MESH)

        return count + other.astype(jnp.int32)

    def greet_workers(n, count):
        count = greet(worker_of(n, home_t, home_w, core), count)
        return lax.cond(h != core, lambda c: greet(worker_of(n, home_t, home_w, h), c), lambda c: c, count)

    greeted = lax.fori_loop(0, HEADS, greet_workers, jnp.int32(0))

    def greet_owners(i, count):
        near_t, kh, near_w = i // 4, i % 2, i // 2 % 2
        owner = tile_of(near_t, kh, near_w)
        for y in range(2):
            count = greet((owner, 2 * y + core), count)

        def others(count):
            for y in range(2):
                count = greet((owner, 2 * y + 1 - core), count)
            return count

        return lax.cond(kh == core, others, lambda count: count, count)

    def greet_all(count):
        count = lax.fori_loop(0, 8, greet_owners, count)
        for device in (sibling, time_near, wide_near):
            count = greet(device, count)
        return count

    greeted = lax.cond(active, greet_all, lambda count: count, greeted)

    copy_in(0).wait()
    copy_in(1).wait()

    @pl.loop(0, HEADS)
    def _(n):
        lanes = lanes_of(n)
        k = k_in[:, lanes].astype(jnp.float32)
        inverse = lax.rsqrt(jnp.mean(k * k, axis=-1, keepdims=True) + EPSILON)
        kv_stage[n, :, 0:HD] = (k * inverse).astype(LOW)
        kv_stage[n, :, HD:] = v_in[:, lanes]

    pl.semaphore_wait(barrier, greeted)

    def send_keys():
        slot = own_t * 2 + own_w
        rows = pl.ds(pl.multiple_of(core * TILE + h * 2 * QUARTER + part // 2 * QUARTER, QUARTER), QUARTER)

        @pl.loop(0, HEADS)
        def _(n):
            copy_to(
                kv_stage.at[n],
                kv.at[slot, rows],
                kv_send,
                kv_recv.at[slot, core],
                worker_of(n, home_t, home_w, core),
                here,
            )

    def send_queries():
        at = query_number(own_t, own_w)

        @pl.loop(0, HEADS)
        def _(n):
            copy_to(
                qg_stage.at[n],
                qg.at[at, quarter(part)],
                qg_send,
                qg_recv,
                worker_of(n, home_t, home_w, h),
                here,
            )

    send_keys()
    copy_in(2).wait()
    copy_in(3).wait()

    @pl.loop(0, HEADS)
    def _(n):
        lanes = lanes_of(n)
        qg_stage[n, :, 0:HD] = q_in[:, lanes]
        qg_stage[n, :, HD:] = g_in[:, lanes]

    send_queries()
    copy_in(4).wait()

    def pass_on(kind, i):
        slot = KINDS[kind][0] + i
        near_t, near_w = pair_at(kind, i)
        arrived(kv.at[slot, half(core)], kv_recv.at[slot, core])

        def send(device, to, sem):
            pltpu.make_async_remote_copy(
                src_ref=kv.at[slot, half(core)],
                dst_ref=kv.at[to, half(core)],
                send_sem=sem,
                recv_sem=kv_recv.at[to, core],
                device_id=device,
                device_id_type=MESH,
            ).start()

        if kind == 0:
            pl.when(near_w == 0)(lambda: send(wide_near, 6 + near_t, wide_send))
        if kind in (0, 2):
            to = 4 + near_w if kind == 0 else 8
            pl.when(near_t == 0)(lambda: send(time_near, to, time_send))
        send(sibling, slot, relay_send)

    def relayed(slot):
        arrived(kv.at[slot, half(1 - core)], kv_recv.at[slot, 1 - core])

    def score_step(kind, i):
        first, count, q0, qn = KINDS[kind]
        slot = first + i
        near_t, near_w = pair_at(kind, i)
        relayed(slot)
        scores = nt(q_unit[q0 * TILE : (q0 + qn) * TILE], kv[slot, :, 0:HD])
        column = lax.broadcasted_iota(jnp.int32, (1, PAIR), 1)
        lower = (column < PAIR // 4) | ((column >= PAIR // 2) & (column < 3 * PAIR // 4))
        lows = []
        for u in range(qn):
            qt, qw = QUERY_AT[q0 + u]
            dt = absolute(T, near_t) - absolute(T, qt)
            dw = absolute(W, near_w) - absolute(W, qw)
            tile = tile_of(qt, core, qw)
            live = [window_ref[tile, 9 * (dt + 1) + 3 * (kh - core + 1) + dw + 1] for kh in range(2)]
            bias = [(one.astype(jnp.float32) - 1.0) * 1e30 for one in live]
            weight = jnp.exp2(scores[u * TILE : (u + 1) * TILE] * (SCALE * LOG2E) + jnp.where(lower, bias[0], bias[1]))
            rows = slice((q0 + u) * TILE, (q0 + u + 1) * TILE)
            total = weight[:, 0:HD]
            for at in range(HD, PAIR, HD):
                total += weight[:, at : at + HD]
            acc[rows, HD:] += total
            lows.append(weight.astype(LOW))
        low = jnp.concatenate(lows, axis=0) if qn > 1 else lows[0]
        weights[kind][i] = low
        acc[q0 * TILE : (q0 + qn) * TILE, 0:HD] += jnp.dot(low, kv[slot, :, HD:], preferred_element_type=jnp.float32)

    def to_sibling(slot):
        return pltpu.make_async_remote_copy(
            src_ref=sib_send.at[slot],
            dst_ref=sib_recv.at[slot],
            send_sem=sib_sent,
            recv_sem=sib_got.at[slot],
            device_id=sibling,
            device_id_type=MESH,
        )

    def send_sum(slot):
        @pl.when(slot < 4)
        def _():
            near_t, near_w = pair_at(0, slot)
            for kh in range(2):
                for y in range(2):
                    copy_to(
                        sum_stage.at[slot, quarter(kh * 2 + y)],
                        dkv_ref.at[head],
                        sum_send,
                        dkv_recv,
                        (tile_of(near_t, kh, near_w), 2 * y + core),
                        here,
                    )

        def pass_back(device):
            pltpu.make_async_remote_copy(
                src_ref=sum_stage.at[slot],
                dst_ref=near_recv.at[slot - 4],
                send_sem=sum_send,
                recv_sem=near_got.at[slot - 4],
                device_id=device,
                device_id_type=MESH,
            ).start()

        wide = (slot == 6) | (slot == 7)
        pl.when(wide)(lambda: pass_back(wide_near))
        pl.when((slot >= 4) & jnp.logical_not(wide))(lambda: pass_back(time_near))

    def taken(g):
        return jnp.where(g < 1, 8, jnp.where(g < 3, 6 - g, jnp.where(g < 5, 10 - g, 8 - g)))

    def finish_sum(g):
        slot = taken(g)
        near_t, near_w = pair_at(0, slot)
        own = slot < 4
        time_at = jnp.where(own & (near_t == 0), near_w, 5)
        wide_at = jnp.where(slot == 6, 4, jnp.where(own & (near_w == 0), 2 + near_t, 5))
        to_sibling(slot).wait_recv()
        for at in (time_at, wide_at):
            pl.when(at < 5)(lambda at=at: arrived(near_recv.at[at], near_got.at[at]))
        total = part_sum[g % (LAG + 1), half(core)] + sib_recv[slot].astype(jnp.float32)
        for at in (time_at, wide_at):
            total += near_recv[at].astype(jnp.float32)
        sum_stage[slot] = total.astype(LOW)
        send_sum(slot)

    def grad_step(kind, g):
        first, count, q0, qn = KINDS[kind]
        slot = taken(g)
        held = g % (LAG + 1)
        rows = slice(q0 * TILE, (q0 + qn) * TILE)
        low = weights[kind][slot - first]
        prob_grad = nt(grad_rows[rows], kv[slot, :, HD:])
        score_grad = (low.astype(jnp.float32) * (prob_grad - repeated(row_dot[rows]))).astype(LOW)
        dq_acc[rows] += jnp.dot(score_grad, kv[slot, :, 0:HD], preferred_element_type=jnp.float32)
        part_sum[held, :, 0:HD] = jnp.dot(scaled[0:HD, rows], score_grad, preferred_element_type=jnp.float32).T
        part_sum[held, :, HD:] = jnp.dot(scaled[HD:, rows], low, preferred_element_type=jnp.float32).T
        sib_send[slot] = part_sum[held, half(1 - core)].astype(LOW)
        to_sibling(slot).start()
        pl.when(g >= LAG)(lambda: finish_sum(g - LAG))

    def send_result(u, stage, dst, send_sem, recv_sem):
        near_t, near_w = u // 2, jnp.where((u == 1) | (u == 2), 0, 1)
        for j in range(4):
            copy_to(
                stage.at[u, quarter(j)],
                dst.at[:, lanes_of(head)],
                send_sem,
                recv_sem,
                (tile_of(near_t, core, near_w), j),
                here,
            )

    @pl.when(active)
    def _():
        acc[...] = jnp.zeros_like(acc)
        dq_acc[...] = jnp.zeros_like(dq_acc)
        near_recv[5] = jnp.zeros((TILE, 2 * HD), LOW)

        pass_on(0, 0)
        pass_on(0, 1)
        pass_on(2, 0)
        arrived(qg, qg_recv)
        for u in range(4):
            q = qg[u, :, 0:HD].astype(jnp.float32)
            inverse = lax.rsqrt(jnp.mean(q * q, axis=-1, keepdims=True) + EPSILON)
            rows = slice(u * TILE, (u + 1) * TILE)
            q_unit[rows] = (q * inverse).astype(LOW)
            grad_rows[rows] = qg[u, :, HD:]

        @pl.loop(0, 4)
        def _(i):
            score_step(0, i)
            pl.when(i < 2)(lambda: pass_on(0, i + 2))
            pl.when(i >= 2)(lambda: pass_on(1, i - 2))

        pass_on(2, 1)
        pass_on(3, 0)

        for kind in (2, 1, 3):

            @pl.loop(0, KINDS[kind][1])
            def _(i):
                score_step(kind, i)

        for u in range(4):
            rows = slice(u * TILE, (u + 1) * TILE)
            over[rows] = jnp.broadcast_to(1.0 / jnp.sum(acc[rows, HD:], axis=-1, keepdims=True), (TILE, HD))
            out = (acc[rows, 0:HD] * over[rows]).astype(LOW)
            o_stage[u] = out
            grad = qg[u, :, HD:].astype(jnp.float32)
            dot = jnp.sum(grad * out.astype(jnp.float32), axis=-1, keepdims=True)
            row_dot[rows] = jnp.broadcast_to(dot, (TILE, HD))
            scaled[0:HD, rows] = (q_unit[rows].astype(jnp.float32) * (over[rows] * SCALE)).T.astype(LOW)
            scaled[HD:, rows] = (grad * over[rows]).T.astype(LOW)

        for kind, start in ((3, 0), (1, 1), (2, 3), (0, 5)):

            @pl.loop(start, start + KINDS[kind][1])
            def _(g):
                grad_step(kind, g)
                if kind in (1, 2):
                    send_result(g - 1, o_stage, o_ref, o_send, o_recv)

        for u in range(4):
            rows = slice(u * TILE, (u + 1) * TILE)
            q = qg[u, :, 0:HD].astype(jnp.float32)
            inverse = lax.rsqrt(jnp.mean(q * q, axis=-1, keepdims=True) + EPSILON)
            unit = q * inverse
            grad_in = dq_acc[rows] * (over[rows] * SCALE)
            dq = inverse * (grad_in - unit * jnp.mean(grad_in * unit, axis=-1, keepdims=True))
            dq_stage[u] = dq.astype(LOW)
        for g in range(SLOTS - LAG, SLOTS):
            finish_sum(g)

        @pl.loop(0, 4)
        def _(u):
            send_result(u, dq_stage, dq_ref, dq_send, dq_recv)

    arrived(dkv_ref, dkv_recv)
    arrived(o_ref, o_recv)
    arrived(dq_ref, dq_recv)

    def left(ref, sem, kept, own):
        pl.when(kept)(lambda: arrived(ref.at[pl.ds(0, own)], sem))
        pl.when(jnp.logical_not(kept))(lambda: arrived(ref, sem))

    left(kv_stage, kv_send, active, HEADS - 1)
    left(qg_stage, qg_send, active & (h == core), HEADS - 1)

    @pl.when(active)
    def _():
        arrived(sib_send, relay_send)
        arrived(sib_send.at[pl.ds(0, 3)], time_send)
        arrived(sib_send.at[pl.ds(0, 2)], wide_send)
        arrived(sib_send, sib_sent)
        arrived(sib_send.at[pl.ds(0, SLOTS - 1)], sum_send)
        arrived(sib_send.at[0, pl.ds(0, 3 * QUARTER)], sum_send)
        for stage, sem in ((o_stage, o_send), (dq_stage, dq_send)):
            arrived(stage.at[pl.ds(0, 3)], sem)
            arrived(stage.at[3, pl.ds(0, 3 * QUARTER)], sem)
            pl.when(h != core)(lambda: arrived(stage.at[3, quarter(3)], sem))


def finish_kernel(o_in, dq_in, dkv_in, k_in, o_ref, dq_ref, dk_ref, dv_ref, o, dq, dkv, k_raw, dk, dv, in_sem, out_sem):
    parts = 3
    heads = HEADS // parts

    def lanes_in(p):
        return slice(p * heads * HD, (p + 1) * heads * HD)

    loads = [(o_in, o), (dq_in, dq)]
    for p in range(parts):
        loads.append((dkv_in.at[p * heads : (p + 1) * heads], dkv.at[p * heads : (p + 1) * heads]))
        loads.append((k_in.at[:, lanes_in(p)], k_raw.at[:, lanes_in(p)]))
    loads = [pltpu.make_async_copy(a, b, in_sem.at[i]) for i, (a, b) in enumerate(loads)]
    stores = [(o, o_ref), (dq, dq_ref)]
    for p in range(parts):
        stores.append((dk.at[:, lanes_in(p)], dk_ref.at[:, lanes_in(p)]))
        stores.append((dv.at[:, lanes_in(p)], dv_ref.at[:, lanes_in(p)]))
    stores = [pltpu.make_async_copy(a, b, out_sem.at[i]) for i, (a, b) in enumerate(stores)]
    for load in loads:
        load.start()
    for i in range(2):
        loads[i].wait()
        stores[i].start()
    for p in range(parts):
        loads[2 + 2 * p].wait()
        loads[3 + 2 * p].wait()
        for n in range(p * heads, (p + 1) * heads):
            lanes = slice(n * HD, (n + 1) * HD)
            k = k_raw[:, lanes].astype(jnp.float32)
            inverse = lax.rsqrt(jnp.mean(k * k, axis=-1, keepdims=True) + EPSILON)
            unit = k * inverse
            grad_in = dkv[n, :, 0:HD].astype(jnp.float32)
            grad = inverse * (grad_in - unit * jnp.mean(grad_in * unit, axis=-1, keepdims=True))
            dk[:, lanes] = grad.astype(LOW)
            dv[:, lanes] = dkv[n, :, HD:]
        stores[2 + 2 * p].start()
        stores[3 + 2 * p].start()
    for store in stores:
        store.wait()


def shards(queries, keys, values, out_grad, window):
    hbm = pl.BlockSpec(memory_space=pl.ANY)
    dma = pltpu.SemaphoreType.DMA
    f32 = jnp.float32
    rows = jax.ShapeDtypeStruct((QUARTER, HEADS * HD), LOW)
    o, dq, dkv = pl.pallas_call(
        attend_kernel,
        out_shape=(rows, rows, jax.ShapeDtypeStruct((HEADS, QUARTER, 2 * HD), LOW)),
        in_specs=[hbm] * 5,
        out_specs=(hbm,) * 3,
        scratch_shapes=[
            pltpu.SMEM(window.shape, window.dtype),
            pltpu.VMEM((QUARTER, HEADS * HD), LOW),
            pltpu.VMEM((QUARTER, HEADS * HD), LOW),
            pltpu.VMEM((QUARTER, HEADS * HD), LOW),
            pltpu.VMEM((QUARTER, HEADS * HD), LOW),
            pltpu.VMEM((HEADS, QUARTER, 2 * HD), LOW),
            pltpu.VMEM((HEADS, QUARTER, 2 * HD), LOW),
            pltpu.VMEM((SLOTS, PAIR, 2 * HD), LOW),
            pltpu.VMEM((4, TILE, 2 * HD), LOW),
            pltpu.VMEM((4 * TILE, HD), LOW),
            pltpu.VMEM((4, 4 * TILE, PAIR), LOW),
            pltpu.VMEM((2, 2 * TILE, PAIR), LOW),
            pltpu.VMEM((2, 2 * TILE, PAIR), LOW),
            pltpu.VMEM((1, TILE, PAIR), LOW),
            pltpu.VMEM((4 * TILE, 2 * HD), f32),
            pltpu.VMEM((4 * TILE, HD), f32),
            pltpu.VMEM((4 * TILE, HD), f32),
            pltpu.VMEM((4 * TILE, HD), f32),
            pltpu.VMEM((2 * HD, 4 * TILE), LOW),
            pltpu.VMEM((4 * TILE, HD), LOW),
            pltpu.VMEM((4, TILE, HD), LOW),
            pltpu.VMEM((4, TILE, HD), LOW),
            pltpu.VMEM((LAG + 1, PAIR, 2 * HD), f32),
            pltpu.VMEM((SLOTS, TILE, 2 * HD), LOW),
            pltpu.VMEM((SLOTS, TILE, 2 * HD), LOW),
            pltpu.VMEM((SLOTS, TILE, 2 * HD), LOW),
            pltpu.VMEM((6, TILE, 2 * HD), LOW),
            dma((5,)),
            pltpu.SemaphoreType.DMA,
            pltpu.SemaphoreType.DMA,
            dma((SLOTS, 2)),
            pltpu.SemaphoreType.DMA,
            pltpu.SemaphoreType.DMA,
            pltpu.SemaphoreType.DMA,
            pltpu.SemaphoreType.DMA,
            pltpu.SemaphoreType.DMA,
            dma((SLOTS,)),
            dma((5,)),
            pltpu.SemaphoreType.DMA,
            pltpu.SemaphoreType.DMA,
            pltpu.SemaphoreType.DMA,
            pltpu.SemaphoreType.DMA,
            pltpu.SemaphoreType.DMA,
            pltpu.SemaphoreType.DMA,
        ],
        compiler_params=pltpu.CompilerParams(collective_id=0, has_side_effects=True, vmem_limit_bytes=VMEM_LIMIT),
        name="attend",
    )(window, queries, keys, values, out_grad)

    return pl.pallas_call(
        finish_kernel,
        out_shape=(rows,) * 4,
        in_specs=[hbm] * 4,
        out_specs=(hbm,) * 4,
        scratch_shapes=[
            pltpu.VMEM((QUARTER, HEADS * HD), LOW),
            pltpu.VMEM((QUARTER, HEADS * HD), LOW),
            pltpu.VMEM((HEADS, QUARTER, 2 * HD), LOW),
            pltpu.VMEM((QUARTER, HEADS * HD), LOW),
            pltpu.VMEM((QUARTER, HEADS * HD), LOW),
            pltpu.VMEM((QUARTER, HEADS * HD), LOW),
            dma((8,)),
            dma((8,)),
        ],
        compiler_params=pltpu.CompilerParams(vmem_limit_bytes=VMEM_LIMIT),
        name="finish",
    )(o, dq, dkv, keys)


def solution(mesh):
    rows = P(("tm", "head"), None)
    return jax.shard_map(
        shards, mesh=mesh, in_specs=(rows, rows, rows, rows, P()), out_specs=(rows, rows, rows, rows), check_vma=False
    )
```

time: 87.1 us -> 83.8 us (0.962); the launches traced: 85.9 us -> 83.6 us
  Pallas kernels: 85.2 us -> 83 us
    pallas_call x1, Pallas kernels: 82.2 us -> 80.4 us  [shards(): pl.pallas_call(attend_kernel, out_shape=(rows, rows, jax.ShapeDtypeStruct...]
where the time goes in v5:
time: 83.8 us; the launch traced here: 83.6 us
  Pallas kernels  83 us (99%)
    pallas_call x1, Pallas kernels, shards(): pl.pallas_call(attend_kernel, out_shape=(rows, rows, jax.ShapeDtypeStruct...  80.4 us
    pallas_call x1, Pallas kernels, shards(): pl.pallas_call(finish_kernel, out_shape=(rows,) * 4, in_specs=[hbm] * 4,...  2.61 us

profile of v5, /device:TPU:29, one launch (start us, length us, event | category | flops | bytes accessed | tf_op | source)
XLA Modules:
  0.0 83.6 jit_solution(11491532495806474624)
XLA Ops:
  0.6 80.4 %attend.1 = (bf16[96,1536]{1,0:T(8,128)(2,1)}, bf16[96,1536]{1,0:T(8,128)(2,1)}, bf16[12,96,256]{2,1,0:T(8,128)(2,1)}) custom-call(s32[32,27]{1,0:T(8,128)} %window_hbm.1, bf16[96,1536]{1,0:T(8,128)(2,1)} %q_hbm.1, bf16[96,1536]{1,0:T(8,128)(2,1)} %k_in.1, bf16[96,1536]{1,0:T(8,128)(2,1)} %v_hbm.1, bf16[96,1536]{1,0:T(8,128)(2,1)} %g_hbm.1), custom_call_target="tpu_custom_call" | custom-call | tf_op jit(solution)/shard_map/attend/pallas_call | solution.py:540
  81.0 2.6 %finish.1 = (bf16[96,1536]{1,0:T(8,128)(2,1)}, bf16[96,1536]{1,0:T(8,128)(2,1)}, bf16[96,1536]{1,0:T(8,128)(2,1)}, bf16[96,1536]{1,0:T(8,128)(2,1)}) custom-call(bf16[96,1536]{1,0:T(8,128)(2,1)} %get-tuple-element.7.o_in, bf16[96,1536]{1,0:T(8,128)(2,1)} %get-tuple-element.8.dq_in, bf16[12,96,256]{2,1,0:T(8,128)(2,1)} %get-tuple-element.9.dkv_in, ...), custom_call_target="tpu_custom_call" | custom-call | tf_op jit(solution)/shard_map/finish/pallas_call | solution.py:595

commit v6 on v5

--- a/solution.py
+++ b/solution.py
@@ -11,7 +11,6 @@
 QUARTER = 96
 PAIR = 768
 SLOTS = 9
-LAG = 1
 EPSILON = 1e-06
 SCALE = HD**-0.5
 LOG2E = 1.4426950408889634
@@ -21,6 +20,7 @@
 
 QUERY_AT = ((0, 1), (0, 0), (1, 0), (1, 1))
 KINDS = ((0, 4, 0, 4), (4, 2, 0, 2), (6, 2, 1, 2), (8, 1, 1, 1))
+FAR = ((3, 0), (2, 1), (1, 1), (2, 0), (1, 0))
 
 
 def worker_of(n, T, W, core):
@@ -112,9 +112,8 @@
     v_in,
     g_in,
     kv_stage,
-    qg_stage,
     kv,
-    qg,
+    q_raw,
     q_unit,
     weights0,
     weights1,
@@ -135,9 +134,11 @@
     near_recv,
     in_sem,
     kv_send,
-    qg_send,
+    q_send,
+    g_send,
     kv_recv,
-    qg_recv,
+    q_recv,
+    g_recv,
     relay_send,
     time_send,
     wide_send,
@@ -238,31 +239,25 @@
                 here,
             )
 
-    def send_queries():
-        at = query_number(own_t, own_w)
+    def send_rows(held, to, send_sem, recv_sem):
+        row = query_number(own_t, own_w) * TILE + part * QUARTER
 
         @pl.loop(0, HEADS)
         def _(n):
             copy_to(
-                qg_stage.at[n],
-                qg.at[at, quarter(part)],
-                qg_send,
-                qg_recv,
+                held.at[:, lanes_of(n)],
+                to.at[pl.ds(pl.multiple_of(row, QUARTER), QUARTER)],
+                send_sem,
+                recv_sem,
                 worker_of(n, home_t, home_w, h),
                 here,
             )
 
     send_keys()
     copy_in(2).wait()
+    send_rows(q_in, q_raw, q_send, q_recv)
     copy_in(3).wait()
-
-    @pl.loop(0, HEADS)
-    def _(n):
-        lanes = lanes_of(n)
-        qg_stage[n, :, 0:HD] = q_in[:, lanes]
-        qg_stage[n, :, HD:] = g_in[:, lanes]
-
-    send_queries()
+    send_rows(g_in, grad_rows, g_send, g_recv)
     copy_in(4).wait()
 
     def pass_on(kind, i):
@@ -356,11 +351,8 @@
         pl.when(wide)(lambda: pass_back(wide_near))
         pl.when((slot >= 4) & jnp.logical_not(wide))(lambda: pass_back(time_near))
 
-    def taken(g):
-        return jnp.where(g < 1, 8, jnp.where(g < 3, 6 - g, jnp.where(g < 5, 10 - g, 8 - g)))
-
-    def finish_sum(g):
-        slot = taken(g)
+    def finish_sum(slot, held):
+        slot = jnp.int32(slot)
         near_t, near_w = pair_at(0, slot)
         own = slot < 4
         time_at = jnp.where(own & (near_t == 0), near_w, 5)
@@ -368,18 +360,17 @@
         to_sibling(slot).wait_recv()
         for at in (time_at, wide_at):
             pl.when(at < 5)(lambda at=at: arrived(near_recv.at[at], near_got.at[at]))
-        total = part_sum[g % (LAG + 1), half(core)] + sib_recv[slot].astype(jnp.float32)
+        total = part_sum[held, half(core)] + sib_recv[slot].astype(jnp.float32)
         for at in (time_at, wide_at):
             total += near_recv[at].astype(jnp.float32)
         sum_stage[slot] = total.astype(LOW)
         send_sum(slot)
 
-    def grad_step(kind, g):
+    def grad_step(kind, i, held):
         first, count, q0, qn = KINDS[kind]
-        slot = taken(g)
-        held = g % (LAG + 1)
+        slot = first + i
         rows = slice(q0 * TILE, (q0 + qn) * TILE)
-        low = weights[kind][slot - first]
+        low = weights[kind][i]
         prob_grad = nt(grad_rows[rows], kv[slot, :, HD:])
         score_grad = (low.astype(jnp.float32) * (prob_grad - repeated(row_dot[rows]))).astype(LOW)
         dq_acc[rows] += jnp.dot(score_grad, kv[slot, :, 0:HD], preferred_element_type=jnp.float32)
@@ -387,7 +378,6 @@
         part_sum[held, :, HD:] = jnp.dot(scaled[HD:, rows], low, preferred_element_type=jnp.float32).T
         sib_send[slot] = part_sum[held, half(1 - core)].astype(LOW)
         to_sibling(slot).start()
-        pl.when(g >= LAG)(lambda: finish_sum(g - LAG))
 
     def send_result(u, stage, dst, send_sem, recv_sem):
         near_t, near_w = u // 2, jnp.where((u == 1) | (u == 2), 0, 1)
@@ -410,13 +400,12 @@
         pass_on(0, 0)
         pass_on(0, 1)
         pass_on(2, 0)
-        arrived(qg, qg_recv)
+        arrived(q_raw, q_recv)
         for u in range(4):
-            q = qg[u, :, 0:HD].astype(jnp.float32)
+            rows = slice(u * TILE, (u + 1) * TILE)
+            q = q_raw[rows].astype(jnp.float32)
             inverse = lax.rsqrt(jnp.mean(q * q, axis=-1, keepdims=True) + EPSILON)
-            rows = slice(u * TILE, (u + 1) * TILE)
             q_unit[rows] = (q * inverse).astype(LOW)
-            grad_rows[rows] = qg[u, :, HD:]
 
         @pl.loop(0, 4)
         def _(i):
@@ -424,49 +413,60 @@
             pl.when(i < 2)(lambda: pass_on(0, i + 2))
             pl.when(i >= 2)(lambda: pass_on(1, i - 2))
 
+        score_step(2, 0)
         pass_on(2, 1)
+
+        @pl.loop(0, 2)
+        def _(i):
+            score_step(1, i)
+
         pass_on(3, 0)
-
-        for kind in (2, 1, 3):
-
-            @pl.loop(0, KINDS[kind][1])
-            def _(i):
-                score_step(kind, i)
+        score_step(2, 1)
+        score_step(3, 0)
+        arrived(grad_rows, g_recv)
 
         for u in range(4):
             rows = slice(u * TILE, (u + 1) * TILE)
             over[rows] = jnp.broadcast_to(1.0 / jnp.sum(acc[rows, HD:], axis=-1, keepdims=True), (TILE, HD))
             out = (acc[rows, 0:HD] * over[rows]).astype(LOW)
             o_stage[u] = out
-            grad = qg[u, :, HD:].astype(jnp.float32)
+            grad = grad_rows[rows].astype(jnp.float32)
             dot = jnp.sum(grad * out.astype(jnp.float32), axis=-1, keepdims=True)
             row_dot[rows] = jnp.broadcast_to(dot, (TILE, HD))
             scaled[0:HD, rows] = (q_unit[rows].astype(jnp.float32) * (over[rows] * SCALE)).T.astype(LOW)
             scaled[HD:, rows] = (grad * over[rows]).T.astype(LOW)
 
-        for kind, start in ((3, 0), (1, 1), (2, 3), (0, 5)):
-
-            @pl.loop(start, start + KINDS[kind][1])
-            def _(g):
-                grad_step(kind, g)
-                if kind in (1, 2):
-                    send_result(g - 1, o_stage, o_ref, o_send, o_recv)
+        def finish_far(at):
+            kind, i = FAR[at]
+            finish_sum(KINDS[kind][0] + i, 4 + at % 2)
+
+        for at, (kind, i) in enumerate(FAR):
+            grad_step(kind, i, 4 + at % 2)
+            if at > 0:
+                finish_far(at - 1)
+                send_result(at - 1, o_stage, o_ref, o_send, o_recv)
+
+        @pl.loop(0, 4)
+        def _(step):
+            grad_step(0, 3 - step, 3 - step)
+            pl.when(step == 0)(lambda: finish_far(4))
+            pl.when(step == 1)(lambda: finish_sum(3, 3))
 
         for u in range(4):
             rows = slice(u * TILE, (u + 1) * TILE)
-            q = qg[u, :, 0:HD].astype(jnp.float32)
+            q = q_raw[rows].astype(jnp.float32)
             inverse = lax.rsqrt(jnp.mean(q * q, axis=-1, keepdims=True) + EPSILON)
             unit = q * inverse
             grad_in = dq_acc[rows] * (over[rows] * SCALE)
             dq = inverse * (grad_in - unit * jnp.mean(grad_in * unit, axis=-1, keepdims=True))
             dq_stage[u] = dq.astype(LOW)
-        for g in range(SLOTS - LAG, SLOTS):
-            finish_sum(g)
-
         @pl.loop(0, 4)
         def _(u):
             send_result(u, dq_stage, dq_ref, dq_send, dq_recv)
 
+        for i in (2, 1, 0):
+            finish_sum(i, i)
+
     arrived(dkv_ref, dkv_recv)
     arrived(o_ref, o_recv)
     arrived(dq_ref, dq_recv)
@@ -476,7 +476,10 @@
         pl.when(jnp.logical_not(kept))(lambda: arrived(ref, sem))
 
     left(kv_stage, kv_send, active, HEADS - 1)
-    left(qg_stage, qg_send, active & (h == core), HEADS - 1)
+    for held, sem in ((q_in, q_send), (g_in, g_send)):
+        kept = active & (h == core)
+        pl.when(kept)(lambda: arrived(held.at[:, 0 : (HEADS - 1) * HD], sem))
+        pl.when(jnp.logical_not(kept))(lambda: arrived(held, sem))
 
     @pl.when(active)
     def _():
@@ -549,9 +552,8 @@
             pltpu.VMEM((QUARTER, HEADS * HD), LOW),
             pltpu.VMEM((QUARTER, HEADS * HD), LOW),
             pltpu.VMEM((HEADS, QUARTER, 2 * HD), LOW),
-            pltpu.VMEM((HEADS, QUARTER, 2 * HD), LOW),
             pltpu.VMEM((SLOTS, PAIR, 2 * HD), LOW),
-            pltpu.VMEM((4, TILE, 2 * HD), LOW),
+            pltpu.VMEM((4 * TILE, HD), LOW),
             pltpu.VMEM((4 * TILE, HD), LOW),
             pltpu.VMEM((4, 4 * TILE, PAIR), LOW),
             pltpu.VMEM((2, 2 * TILE, PAIR), LOW),
@@ -565,7 +567,7 @@
             pltpu.VMEM((4 * TILE, HD), LOW),
             pltpu.VMEM((4, TILE, HD), LOW),
             pltpu.VMEM((4, TILE, HD), LOW),
-            pltpu.VMEM((LAG + 1, PAIR, 2 * HD), f32),
+            pltpu.VMEM((6, PAIR, 2 * HD), f32),
             pltpu.VMEM((SLOTS, TILE, 2 * HD), LOW),
             pltpu.VMEM((SLOTS, TILE, 2 * HD), LOW),
             pltpu.VMEM((SLOTS, TILE, 2 * HD), LOW),
@@ -573,7 +575,9 @@
             dma((5,)),
             pltpu.SemaphoreType.DMA,
             pltpu.SemaphoreType.DMA,
+            pltpu.SemaphoreType.DMA,
             dma((SLOTS, 2)),
+            pltpu.SemaphoreType.DMA,
             pltpu.SemaphoreType.DMA,
             pltpu.SemaphoreType.DMA,
             pltpu.SemaphoreType.DMA,

time: 83.8 us -> 80.8 us (0.964)
  the two profiles are of different devices: /device:TPU:29 before, /device:TPU:18 now
where the time goes in v6:
time: 80.8 us; the launch traced here: 80.6 us
  Pallas kernels  79.8 us (99%)
  between operations  0.82 us (1%)
    pallas_call x1, Pallas kernels, shards(): pl.pallas_call(attend_kernel, out_shape=(rows, rows, jax.ShapeDtypeStruct...  77.2 us
    pallas_call x1, Pallas kernels, shards(): pl.pallas_call(finish_kernel, out_shape=(rows,) * 4, in_specs=[hbm] * 4,...  2.61 us

profile of v6, /device:TPU:18, one launch (start us, length us, event | category | flops | bytes accessed | tf_op | source)
XLA Modules:
  0.0 80.6 jit_solution(7565312977403400799)
XLA Ops:
  0.6 77.2 %attend.1 = (bf16[96,1536]{1,0:T(8,128)(2,1)}, bf16[96,1536]{1,0:T(8,128)(2,1)}, bf16[12,96,256]{2,1,0:T(8,128)(2,1)}) custom-call(s32[32,27]{1,0:T(8,128)} %window_hbm.1, bf16[96,1536]{1,0:T(8,128)(2,1)} %q_hbm.1, bf16[96,1536]{1,0:T(8,128)(2,1)} %k_in.1, bf16[96,1536]{1,0:T(8,128)(2,1)} %v_hbm.1, bf16[96,1536]{1,0:T(8,128)(2,1)} %g_hbm.1), custom_call_target="tpu_custom_call" | custom-call | tf_op jit(solution)/shard_map/attend/pallas_call | solution.py:543
  77.9 2.6 %finish.1 = (bf16[96,1536]{1,0:T(8,128)(2,1)}, bf16[96,1536]{1,0:T(8,128)(2,1)}, bf16[96,1536]{1,0:T(8,128)(2,1)}, bf16[96,1536]{1,0:T(8,128)(2,1)}) custom-call(bf16[96,1536]{1,0:T(8,128)(2,1)} %get-tuple-element.7.o_in, bf16[96,1536]{1,0:T(8,128)(2,1)} %get-tuple-element.8.dq_in, bf16[12,96,256]{2,1,0:T(8,128)(2,1)} %get-tuple-element.9.dkv_in, ...), custom_call_target="tpu_custom_call" | custom-call | tf_op jit(solution)/shard_map/finish/pallas_call | solution.py:599

commit v7 on v6

--- a/solution.py
+++ b/solution.py
@@ -188,7 +188,7 @@
         count = greet(worker_of(n, home_t, home_w, core), count)
         return lax.cond(h != core, lambda c: greet(worker_of(n, home_t, home_w, h), c), lambda c: c, count)
 
-    greeted = lax.fori_loop(0, HEADS, greet_workers, jnp.int32(0))
+    greeted = lax.fori_loop(0, HEADS, greet_workers, jnp.int32(0), unroll=True)
 
     def greet_owners(i, count):
         near_t, kh, near_w = i // 4, i % 2, i // 2 % 2
@@ -204,7 +204,7 @@
         return lax.cond(kh == core, others, lambda count: count, count)
 
     def greet_all(count):
-        count = lax.fori_loop(0, 8, greet_owners, count)
+        count = lax.fori_loop(0, 8, greet_owners, count, unroll=True)
         for device in (sibling, time_near, wide_near):
             count = greet(device, count)
         return count
@@ -228,7 +228,7 @@
         slot = own_t * 2 + own_w
         rows = pl.ds(pl.multiple_of(core * TILE + h * 2 * QUARTER + part // 2 * QUARTER, QUARTER), QUARTER)
 
-        @pl.loop(0, HEADS)
+        @pl.loop(0, HEADS, unroll=True)
         def _(n):
             copy_to(
                 kv_stage.at[n],
@@ -242,7 +242,7 @@
     def send_rows(held, to, send_sem, recv_sem):
         row = query_number(own_t, own_w) * TILE + part * QUARTER
 
-        @pl.loop(0, HEADS)
+        @pl.loop(0, HEADS, unroll=True)
         def _(n):
             copy_to(
                 held.at[:, lanes_of(n)],
@@ -253,12 +253,20 @@
                 here,
             )
 
-    send_keys()
     copy_in(2).wait()
     send_rows(q_in, q_raw, q_send, q_recv)
+    send_keys()
     copy_in(3).wait()
-    send_rows(g_in, grad_rows, g_send, g_recv)
     copy_in(4).wait()
+
+    def send_grads():
+        send_rows(g_in, grad_rows, g_send, g_recv)
+
+    @pl.when(jnp.logical_not(active))
+    def _():
+        arrived(kv_stage, kv_send)
+        send_grads()
+
 
     def pass_on(kind, i):
         slot = KINDS[kind][0] + i
@@ -400,6 +408,7 @@
         pass_on(0, 0)
         pass_on(0, 1)
         pass_on(2, 0)
+        send_grads()
         arrived(q_raw, q_recv)
         for u in range(4):
             rows = slice(u * TILE, (u + 1) * TILE)
@@ -460,8 +469,6 @@
             grad_in = dq_acc[rows] * (over[rows] * SCALE)
             dq = inverse * (grad_in - unit * jnp.mean(grad_in * unit, axis=-1, keepdims=True))
             dq_stage[u] = dq.astype(LOW)
-        @pl.loop(0, 4)
-        def _(u):
             send_result(u, dq_stage, dq_ref, dq_send, dq_recv)
 
         for i in (2, 1, 0):
@@ -471,11 +478,7 @@
     arrived(o_ref, o_recv)
     arrived(dq_ref, dq_recv)
 
-    def left(ref, sem, kept, own):
-        pl.when(kept)(lambda: arrived(ref.at[pl.ds(0, own)], sem))
-        pl.when(jnp.logical_not(kept))(lambda: arrived(ref, sem))
-
-    left(kv_stage, kv_send, active, HEADS - 1)
+    pl.when(active)(lambda: arrived(kv_stage.at[pl.ds(0, HEADS - 1)], kv_send))
     for held, sem in ((q_in, q_send), (g_in, g_send)):
         kept = active & (h == core)
         pl.when(kept)(lambda: arrived(held.at[:, 0 : (HEADS - 1) * HD], sem))

time: 80.8 us -> 78.7 us (0.974)
  the two profiles are of different devices: /device:TPU:18 before, /device:TPU:90 now
where the time goes in v7:
time: 78.7 us; the launch traced here: 78.5 us
  Pallas kernels  77.7 us (99%)
  between operations  0.82 us (1%)
    pallas_call x1, Pallas kernels, shards(): pl.pallas_call(attend_kernel, out_shape=(rows, rows, jax.ShapeDtypeStruct...  75.1 us
    pallas_call x1, Pallas kernels, shards(): pl.pallas_call(finish_kernel, out_shape=(rows,) * 4, in_specs=[hbm] * 4,...  2.61 us

profile of v7, /device:TPU:90, one launch (start us, length us, event | category | flops | bytes accessed | tf_op | source)
XLA Modules:
  0.0 78.5 jit_solution(10683345646303859342)
XLA Ops:
  0.6 75.1 %attend.1 = (bf16[96,1536]{1,0:T(8,128)(2,1)}, bf16[96,1536]{1,0:T(8,128)(2,1)}, bf16[12,96,256]{2,1,0:T(8,128)(2,1)}) custom-call(s32[32,27]{1,0:T(8,128)} %window_hbm.1, bf16[96,1536]{1,0:T(8,128)(2,1)} %q_hbm.1, bf16[96,1536]{1,0:T(8,128)(2,1)} %k_in.1, bf16[96,1536]{1,0:T(8,128)(2,1)} %v_hbm.1, bf16[96,1536]{1,0:T(8,128)(2,1)} %g_hbm.1), custom_call_target="tpu_custom_call" | custom-call | tf_op jit(solution)/shard_map/attend/pallas_call | solution.py:546
  75.8 2.6 %finish.1 = (bf16[96,1536]{1,0:T(8,128)(2,1)}, bf16[96,1536]{1,0:T(8,128)(2,1)}, bf16[96,1536]{1,0:T(8,128)(2,1)}, bf16[96,1536]{1,0:T(8,128)(2,1)}) custom-call(bf16[96,1536]{1,0:T(8,128)(2,1)} %get-tuple-element.7.o_in, bf16[96,1536]{1,0:T(8,128)(2,1)} %get-tuple-element.8.dq_in, bf16[12,96,256]{2,1,0:T(8,128)(2,1)} %get-tuple-element.9.dkv_in, ...), custom_call_target="tpu_custom_call" | custom-call | tf_op jit(solution)/shard_map/finish/pallas_call | solution.py:602

commit v8 on v7

--- a/solution.py
+++ b/solution.py
@@ -20,7 +20,7 @@
 
 QUERY_AT = ((0, 1), (0, 0), (1, 0), (1, 1))
 KINDS = ((0, 4, 0, 4), (4, 2, 0, 2), (6, 2, 1, 2), (8, 1, 1, 1))
-FAR = ((3, 0), (2, 1), (1, 1), (2, 0), (1, 0))
+FAR = ((3, 0), (2, 1), (1, 1), (1, 0), (2, 0))
 
 
 def worker_of(n, T, W, core):

time: 78.7 us -> 76.9 us (0.977)
  the two profiles are of different devices: /device:TPU:90 before, /device:TPU:108 now
where the time goes in v8:
time: 76.9 us; the launch traced here: 76.8 us
  Pallas kernels  75.9 us (99%)
  between operations  0.82 us (1%)
    pallas_call x1, Pallas kernels, shards(): pl.pallas_call(attend_kernel, out_shape=(rows, rows, jax.ShapeDtypeStruct...  73.3 us
    pallas_call x1, Pallas kernels, shards(): pl.pallas_call(finish_kernel, out_shape=(rows,) * 4, in_specs=[hbm] * 4,...  2.61 us

profile of v8, /device:TPU:108, one launch (start us, length us, event | category | flops | bytes accessed | tf_op | source)
XLA Modules:
  0.0 76.8 jit_solution(15437705858158625892)
XLA Ops:
  0.6 73.3 %attend.1 = (bf16[96,1536]{1,0:T(8,128)(2,1)}, bf16[96,1536]{1,0:T(8,128)(2,1)}, bf16[12,96,256]{2,1,0:T(8,128)(2,1)}) custom-call(s32[32,27]{1,0:T(8,128)} %window_hbm.1, bf16[96,1536]{1,0:T(8,128)(2,1)} %q_hbm.1, bf16[96,1536]{1,0:T(8,128)(2,1)} %k_in.1, bf16[96,1536]{1,0:T(8,128)(2,1)} %v_hbm.1, bf16[96,1536]{1,0:T(8,128)(2,1)} %g_hbm.1), custom_call_target="tpu_custom_call" | custom-call | tf_op jit(solution)/shard_map/attend/pallas_call | solution.py:546
  74.0 2.6 %finish.1 = (bf16[96,1536]{1,0:T(8,128)(2,1)}, bf16[96,1536]{1,0:T(8,128)(2,1)}, bf16[96,1536]{1,0:T(8,128)(2,1)}, bf16[96,1536]{1,0:T(8,128)(2,1)}) custom-call(bf16[96,1536]{1,0:T(8,128)(2,1)} %get-tuple-element.7.o_in, bf16[96,1536]{1,0:T(8,128)(2,1)} %get-tuple-element.8.dq_in, bf16[12,96,256]{2,1,0:T(8,128)(2,1)} %get-tuple-element.9.dkv_in, ...), custom_call_target="tpu_custom_call" | custom-call | tf_op jit(solution)/shard_map/finish/pallas_call | solution.py:602

commit v9 on v8

--- a/solution.py
+++ b/solution.py
@@ -449,17 +449,19 @@
             kind, i = FAR[at]
             finish_sum(KINDS[kind][0] + i, 4 + at % 2)
 
+        grad_step(0, 3, 3)
         for at, (kind, i) in enumerate(FAR):
             grad_step(kind, i, 4 + at % 2)
+            if at == 0:
+                finish_sum(3, 3)
             if at > 0:
                 finish_far(at - 1)
                 send_result(at - 1, o_stage, o_ref, o_send, o_recv)
 
-        @pl.loop(0, 4)
+        @pl.loop(0, 3)
         def _(step):
-            grad_step(0, 3 - step, 3 - step)
+            grad_step(0, 2 - step, 2 - step)
             pl.when(step == 0)(lambda: finish_far(4))
-            pl.when(step == 1)(lambda: finish_sum(3, 3))
 
         for u in range(4):
             rows = slice(u * TILE, (u + 1) * TILE)

time: 76.9 us -> 77.9 us (1.013)
  the two profiles are of different devices: /device:TPU:108 before, /device:TPU:29 now
where the time goes in v9:
time: 77.9 us; the launch traced here: 76.8 us
  Pallas kernels  76 us (98%)
  between operations  0.82 us (1%)
    pallas_call x1, Pallas kernels, shards(): pl.pallas_call(attend_kernel, out_shape=(rows, rows, jax.ShapeDtypeStruct...  73.4 us
    pallas_call x1, Pallas kernels, shards(): pl.pallas_call(finish_kernel, out_shape=(rows,) * 4, in_specs=[hbm] * 4,...  2.61 us

profile of v9, /device:TPU:29, one launch (start us, length us, event | category | flops | bytes accessed | tf_op | source)
XLA Modules:
  0.0 76.8 jit_solution(13414649532655526564)
XLA Ops:
  0.6 73.4 %attend.1 = (bf16[96,1536]{1,0:T(8,128)(2,1)}, bf16[96,1536]{1,0:T(8,128)(2,1)}, bf16[12,96,256]{2,1,0:T(8,128)(2,1)}) custom-call(s32[32,27]{1,0:T(8,128)} %window_hbm.1, bf16[96,1536]{1,0:T(8,128)(2,1)} %q_hbm.1, bf16[96,1536]{1,0:T(8,128)(2,1)} %k_in.1, bf16[96,1536]{1,0:T(8,128)(2,1)} %v_hbm.1, bf16[96,1536]{1,0:T(8,128)(2,1)} %g_hbm.1), custom_call_target="tpu_custom_call" | custom-call | tf_op jit(solution)/shard_map/attend/pallas_call | solution.py:548
  74.0 2.6 %finish.1 = (bf16[96,1536]{1,0:T(8,128)(2,1)}, bf16[96,1536]{1,0:T(8,128)(2,1)}, bf16[96,1536]{1,0:T(8,128)(2,1)}, bf16[96,1536]{1,0:T(8,128)(2,1)}) custom-call(bf16[96,1536]{1,0:T(8,128)(2,1)} %get-tuple-element.7.o_in, bf16[96,1536]{1,0:T(8,128)(2,1)} %get-tuple-element.8.dq_in, bf16[12,96,256]{2,1,0:T(8,128)(2,1)} %get-tuple-element.9.dkv_in, ...), custom_call_target="tpu_custom_call" | custom-call | tf_op jit(solution)/shard_map/finish/pallas_call | solution.py:604
